TPU v7x, 32 devices: a whole 2x2x4 slice. The times are simulated.
32 devices in a mesh: cfg: 2 (over x), sx: 16 (over z, y, core).
Axes of the slice: x: 2, y: 2, z: 4, core: 2. Of those that a mesh axis runs over, the one named last changes fastest.
Arguments:
- eigvecs: bfloat16 [512, 2, 3, 16, 1024], P('cfg', None, None, 'sx'), parts along dimension 0, may hold values from -6 to 6
- link_seed: int32 [6], P('cfg'), parts along dimension 0, may hold values from 1 to 46336
- ownership: int32 [2080], replicated, may hold values from 0 to 2079, each once
Outputs:
- elementals: float32 [4160, 96], P(('cfg', 'sx')), parts along dimension 0
There are 2 independent parts, one for each index of `cfg`. A program takes and returns all parts, laid end to end along the dimension named above; an argument that names none is the same for every part. Nothing has to cross between parts.
Inputs may be any that keep to these rules, and one draw needn't show every extreme that they name: ownership is a permutation of the pair tiles 0 to 2079.
All inputs are finite; a program needn't handle non-finite values.
Results may differ from a plain program's by a relative error of at most 0.0029.
Values may be sent and summed in bfloat16 or wider, within the bound.
No kernel may reach another device: no remote copies, remote signals or barrier semaphores. Data moves between devices by JAX's collectives and lax.ppermute only.
A program may use at most 192 MiB of HBM per device.

v0:
```python
import functools
import math

import jax
import jax.numpy as jnp
from jax import lax
from jax.experimental import pallas as pl
from jax.experimental.pallas import tpu as pltpu
from jax.sharding import PartitionSpec as P

TM = 4
NZ = 64
LANES = 128
MODULUS = 46337
STEP = 32
F32 = jnp.float32
BF16 = jnp.bfloat16
NT = (((1,), (1,)), ((), ()))


def dot(left, right, dims=(((1,), (0,)), ((), ()))):
    return lax.dot_general(left, right, dims, preferred_element_type=F32)


def iota(shape, axis):
    return lax.broadcasted_iota(jnp.int32, shape, axis)


def round_up(value, step):
    return -(-value // step) * step


def divide(value):
    quotient = (value.astype(F32) * (1.0 / MODULUS)).astype(jnp.int32)
    rest = value - quotient * MODULUS
    below, above = rest < 0, rest >= MODULUS
    rest = jnp.where(below, rest + MODULUS, jnp.where(above, rest - MODULUS, rest))
    quotient = jnp.where(below, quotient - 1, jnp.where(above, quotient + 1, quotient))
    return quotient, rest


def link_angles(seed, site):
    high, low = divide(site)
    mixed = divide(seed * seed + low)[1]
    mixed = divide(mixed * mixed + high * 977 + 31)[1]
    angles = []
    for index in range(7):
        g = divide(mixed + (5171 * index + 1))[1]
        g = divide(g * g + low)[1]
        g = divide(g * g + 12345)[1]
        angles.append(g.astype(F32) * (2.0 * math.pi / MODULUS) - math.pi)
    return angles


def store_links(u_ref, seed, site):
    a = link_angles(seed, site)
    ca, sa = jnp.cos(a[0]), jnp.sin(a[0])
    cb, sb = jnp.cos(a[1]), jnp.sin(a[1])
    cg, sg = jnp.cos(a[2]), jnp.sin(a[2])
    rotation = [
        [ca * cb * cg - sa * sg, -ca * cb * sg - sa * cg, ca * sb],
        [sa * cb * cg + ca * sg, -sa * cb * sg + ca * cg, sa * sb],
        [-sb * cg, sb * sg, cb],
    ]
    left = [a[3], a[4], -a[3] - a[4]]
    right = [a[5], a[6], -a[5] - a[6]]
    for c in range(3):
        for s in range(3):
            phase = left[c] + right[s]
            u_ref[2 * (3 * c + s)] = rotation[c][s] * jnp.cos(phase)
            u_ref[2 * (3 * c + s) + 1] = rotation[c][s] * jnp.sin(phase)


def hop(vector_ref, out_ref, u_ref, first, count):
    all_modes, plane = vector_ref.shape[0] // 2, vector_ref.shape[1] // 3
    wide = (STEP // 8, 8, LANES)
    for t in range(plane // LANES):
        u = [jnp.broadcast_to(u_ref[k, t : t + 1, :], (8, LANES)) for k in range(18)]

        def body(block, carry, t=t, u=u):
            rows = [
                pl.ds(pl.multiple_of(part * all_modes + first + block * STEP, STEP), STEP)
                for part in range(2)
            ]
            lanes = [slice(c * plane + t * LANES, c * plane + (t + 1) * LANES) for c in range(3)]
            v = [
                [vector_ref[rows[part], lanes[c]].astype(F32).reshape(wide) for part in range(2)]
                for c in range(3)
            ]
            for c in range(3):
                real = imag = None
                for s in range(3):
                    ur, ui = u[2 * (3 * c + s)], u[2 * (3 * c + s) + 1]
                    re, im = v[s]
                    real = ur * re if real is None else real + ur * re
                    real = real - ui * im
                    imag = ur * im if imag is None else imag + ur * im
                    imag = imag + ui * re
                for part, value in ((0, real), (1, imag)):
                    out_ref[rows[part], lanes[c]] = value.reshape(STEP, LANES).astype(BF16)
            return carry

        lax.fori_loop(0, count // STEP, body, 0)


def products(left_ref, hop_ref):
    n, modes = left_ref.shape[0] // 2, hop_ref.shape[0] // 2
    by_real = dot(left_ref[:n, :], hop_ref[...], NT)
    by_imag = dot(left_ref[n:, :], hop_ref[...], NT)
    if modes % LANES:
        crossed = pltpu.roll(by_imag, modes, 1)
        low = iota(crossed.shape, 1) < modes
        return jnp.where(low, by_real + crossed, by_real - crossed)
    real = by_real[:, :modes] + by_imag[:, modes:]
    imag = by_real[:, modes:] - by_imag[:, :modes]
    return real, imag


class Slots:
    LOW = 2 * LANES

    def __init__(self, all_modes, slots):
        self.tiles = all_modes // TM
        assert 2 * self.tiles == LANES
        self.half = self.tiles // 2
        self.columns = 2 * TM * TM
        self.high = self.half * self.tiles // self.LOW
        assert self.high * self.columns == self.LOW
        self.depth = self.LOW + LANES
        self.groups = LANES // self.columns
        self.per_group = -(-slots // self.groups)
        self.rows = round_up(self.per_group, 8)
        self.all_rows = round_up(self.groups * self.rows, 16)
        assert self.all_rows == self.groups * self.rows

    def codes(self, pair):
        n = self.tiles

        def start(i):
            return i * n - (i * (i - 1)) // 2

        inside = ((2 * n + 1) ** 2 - 8 * pair).astype(F32)
        i = ((2 * n + 1 - jnp.sqrt(inside)) * 0.5).astype(jnp.int32)
        i = jnp.where(start(i) > pair, i - 1, i)
        i = jnp.where(start(i + 1) <= pair, i + 1, i)
        j = i + pair - start(i)
        first = i < self.half
        place = jnp.where(first, i * n + j, (n - 1 - i) * n + (n - 1 - j))
        corner = jnp.logical_and(jnp.logical_not(first), i == j)
        high = jnp.where(corner, 0, place // self.LOW)
        low = jnp.where(corner, self.LOW + (n - 1 - i), place % self.LOW)
        return high * 512 + low

    def arrange(self, codes):
        devices, slots = codes.shape
        spread = jnp.pad(
            codes, ((0, 0), (0, self.groups * self.per_group - slots)), constant_values=-1
        ).reshape(devices, self.groups, self.per_group)
        spread = jnp.pad(
            spread, ((0, 0), (0, 0), (0, self.rows - self.per_group)), constant_values=-1
        )
        return spread.reshape(devices, self.all_rows).T


def store_table(table_ref, fold_ref, real, imag, slots):
    all_modes = real.shape[0]
    n, half = slots.tiles, slots.half
    parts = [real - real.T, imag + imag.T]

    def choose(count, width, turned):
        row, column = iota((count, all_modes), 0), iota((count, all_modes), 1)
        r, i = row // width, row % width
        if turned:
            i = n - 1 - i
        return (column == i * TM + r).astype(F32).astype(BF16)

    pick = [choose(TM * half, half, turned) for turned in (False, True)]
    spread = [choose(all_modes, n, turned) for turned in (False, True)]
    row_i = iota((TM * half, all_modes), 0) % half
    lane_j = iota((TM * half, all_modes), 1) % n
    corners = []
    for part in range(2):
        entries = parts[part].astype(BF16)
        straight, turned = [
            dot(dot(pick[k], entries).astype(BF16), spread[k], NT) for k in range(2)
        ]
        folded = jnp.where(lane_j >= row_i, straight, turned)
        for k in range(TM // 2):
            fold_ref[k, part * TM * half : (part + 1) * TM * half, :] = folded[
                :, k * LANES : (k + 1) * LANES
            ]
        diagonal = jnp.where(lane_j == row_i, turned, 0.0)
        for r in range(TM):
            corners.append(
                jnp.sum(diagonal[r * half : (r + 1) * half], axis=0, keepdims=True)
            )
    low = iota((2 * TM, LANES), 1) < n

    def split(even, odd, high, lanes):
        for pair in range(TM // 2):
            e, o = even[pair], odd[pair]
            top = high * slots.columns + 2 * pair * 2 * TM
            table_ref[top : top + 2 * TM, lanes] = jnp.where(low, e, pltpu.roll(o, n, 1))
            table_ref[top + 2 * TM : top + 4 * TM, lanes] = jnp.where(
                low, pltpu.roll(e, n, 1), o
            )

    halves = [slice(k * LANES, (k + 1) * LANES) for k in range(TM // 2)]
    for two in range(half // 2):
        even = [fold_ref[k, pl.ds(2 * two, 2 * TM, stride=half), :] for k in range(TM // 2)]
        odd = [fold_ref[k, pl.ds(2 * two + 1, 2 * TM, stride=half), :] for k in range(TM // 2)]
        at = two * LANES % slots.LOW
        split(even, odd, two * LANES // slots.LOW, slice(at, at + LANES))
    corner = jnp.concatenate(corners, 0)
    nothing = jnp.zeros((2 * TM, LANES), F32)
    table_ref[:, slots.LOW :] = jnp.zeros((slots.LOW, LANES), F32)
    split([corner[:, h] for h in halves], [nothing] * len(halves), 0, slice(slots.LOW, slots.depth))


def pick_tiles(emit, owner_ref, tables, chosen_ref, slots):
    inside, column = iota((slots.LOW, LANES), 0) % slots.columns, iota((slots.LOW, LANES), 1)
    entry = (inside % (2 * TM)) * TM + inside // (2 * TM)
    fold = (column % slots.columns == entry).astype(F32).astype(BF16)
    rows = slots.all_rows
    lane16 = iota((16, LANES), 1)
    lanes = [
        (lane16 + t * LANES).astype(jnp.int16) for t in range(slots.depth // LANES)
    ]
    one, zero = jnp.ones((16, LANES), BF16), jnp.zeros((16, LANES), BF16)
    lane_group = iota((slots.rows, LANES), 1) // slots.columns
    high_group = iota((rows, LANES), 1) // slots.columns
    count = owner_ref.shape[1] // 2
    for half in range(2):
        high = []
        for k in range(count):
            n = half * count + k
            code = jnp.broadcast_to(owner_ref[:, n : n + 1], (rows, LANES))
            high.append(code >> 9)
            low = (code & 511).astype(jnp.int16)
            for top in range(0, rows, 16):
                for t in range(slots.depth // LANES):
                    chosen_ref[
                        half, k * rows + top : k * rows + top + 16, t * LANES : (t + 1) * LANES
                    ] = jnp.where(low[top : top + 16] == lanes[t], one, zero)
        for d, table in enumerate(tables):
            parts = dot(chosen_ref[half], table, NT)
            masked = jnp.concatenate(
                [
                    jnp.concatenate(
                        [
                            jnp.where(
                                high[k] == high_group + side * slots.groups,
                                parts[k * rows : (k + 1) * rows, side * LANES : (side + 1) * LANES],
                                0.0,
                            )
                            for side in range(2)
                        ],
                        1,
                    ).astype(BF16)
                    for k in range(count)
                ],
                0,
            )
            picked = dot(masked, fold)
            for k in range(count):
                top = k * rows
                packed = picked[top : top + slots.rows]
                for g in range(1, slots.groups):
                    piece = picked[top + g * slots.rows : top + (g + 1) * slots.rows]
                    packed = jnp.where(lane_group == g, piece, packed)
                emit(half * count + k, d, packed)


def store_all_links(links_ref, seed_ref, x):
    _, _, tiles, _ = links_ref.shape
    plane = tiles * LANES
    place = iota((tiles, LANES), 0) * LANES + iota((tiles, LANES), 1)
    before_y = jnp.where(place < NZ, place + (plane - NZ), place - NZ)
    before_z = jnp.where(place % NZ == 0, place + (NZ - 1), place - 1)
    for d, source in enumerate((place, before_y, before_z)):
        store_links(links_ref.at[d], seed_ref[d], source + x * plane)


def load_modes(planar_hbm, out_ref, sems, first):
    _, _, count, plane = planar_hbm.shape
    modes = out_ref.shape[0] // 2
    copies = [
        pltpu.make_async_copy(
            planar_hbm.at[c, part],
            out_ref.at[pl.ds(part * modes + first, count), pl.ds(c * plane, plane)],
            sems.at[2 * c + part],
        )
        for c in range(3)
        for part in range(2)
    ]
    for copy in copies:
        copy.start()
    return copies


def load_all(parts, out_ref, sems):
    quarter = out_ref.shape[0] // 8
    copies = []
    for k, (first, _) in enumerate(chunks_of(4 * quarter)):
        copies += load_modes(parts[k], out_ref, sems.at[k], first)
    return copies


def wait_all(copies):
    for copy in copies:
        copy.wait()


def store_left_y(out_ref, left_ref, plane):
    wide = 2 * LANES
    source, target = iota((wide, wide), 0), iota((wide, wide), 1)
    halves = source == (target // LANES) * LANES + (target + NZ) % LANES
    halves = halves.astype(F32).astype(BF16)
    low = iota((left_ref.shape[0], LANES), 1) < NZ
    for c in range(3):
        swapped = []
        for start in range(c * plane, (c + 1) * plane, wide):
            both = dot(left_ref[:, start : start + wide], halves)
            swapped += [both[:, :LANES], both[:, LANES:]]
        for t in range(plane // LANES):
            lanes = slice(c * plane + t * LANES, c * plane + (t + 1) * LANES)
            out_ref[:, lanes] = jnp.where(low, swapped[t - 1], swapped[t]).astype(BF16)


def store_left_z(out_ref, left_ref, plane):
    wide = 2 * LANES
    source, target = iota((wide, wide), 0), iota((wide, wide), 1)
    before = jnp.where(target % NZ == 0, target + (NZ - 1), target - 1)
    behind = (source == before).astype(F32).astype(BF16)
    for start in range(0, 3 * plane, wide):
        piece = dot(left_ref[:, start : start + wide], behind)
        out_ref[:, start : start + wide] = piece.astype(BF16)


def load_kernel(starts, whole_hbm, *refs):
    parts, sems = refs[-1 - len(starts) : -1], refs[-1]
    copies = [
        pltpu.make_async_copy(whole_hbm.at[pl.ds(start, part.shape[0])], part, sems.at[k])
        for k, (start, part) in enumerate(zip(starts, parts))
    ]
    for copy in copies:
        copy.start()
    wait_all(copies)


def place_of(n, here, near, far):
    return lax.rem(n % near + near - lax.rem(here, near), near) * far + n // near


def inner_kernel(
    slots,
    grid,
    seed_ref,
    where_ref,
    owner_ref,
    a,
    b,
    c,
    *refs,
):
    near, far = grid
    sent, refs = refs[:near], refs[near:]
    links_x_ref, vector_ref, left_ref, hop_ref, links_ref, *refs = refs
    table_ref, fold_ref, chosen_ref, stage_ref, sems = refs
    modes, plane = vector_ref.shape[0] // 2, vector_ref.shape[1] // 3
    copies = load_all((a, b, c), vector_ref, sems)
    store_all_links(links_ref, seed_ref, where_ref[0])
    links_x_ref[...] = links_ref[0]
    wait_all(copies)
    tables = []
    for d, store_left in ((1, store_left_y), (2, store_left_z)):
        store_left(left_ref, vector_ref, plane)
        hop(vector_ref, hop_ref, links_ref.at[d], 0, modes)
        real, imag = products(left_ref, hop_ref)
        store_table(table_ref.at[d - 1], fold_ref, real, imag, slots)
        tables.append(table_ref.at[d - 1])

    def emit(n, d, packed):
        stage_ref[place_of(n, where_ref[0], near, far), d] = packed.astype(BF16)

    pick_tiles(emit, owner_ref, [t[...].astype(BF16) for t in tables], chosen_ref, slots)
    for k in range(near):
        sent[k][...] = stage_ref[k * far : (k + 1) * far]


def outer_chunk(links_ref, upper_hbm, own_hbm, vector_ref, left_ref, hop_ref, sems):
    arriving = load_modes(upper_hbm, vector_ref, sems.at[3], 0)
    own = load_all(own_hbm, left_ref, sems)
    wait_all(arriving)
    hop(vector_ref, hop_ref, links_ref, 0, vector_ref.shape[0] // 2)
    wait_all(own)
    return products(left_ref, hop_ref)


def wide_kernel(links_ref, upper_hbm, a, b, c, out_ref, *scratch):
    out_ref[0], out_ref[1] = outer_chunk(links_ref, upper_hbm, (a, b, c), *scratch)


def narrow_kernel(links_ref, upper_hbm, a, b, c, before_hbm, out_ref, *scratch):
    del before_hbm
    out_ref[...] = outer_chunk(links_ref, upper_hbm, (a, b, c), *scratch)


def last_kernel(
    slots,
    grid,
    where_ref,
    owner_ref,
    first_ref,
    second_ref,
    links_ref,
    upper_hbm,
    a,
    b,
    c,
    *refs,
):
    near, far = grid
    sent_hbm, refs = refs[:near], refs[near:]
    vector_ref, left_ref, hop_ref, sems, table_ref, fold_ref, chosen_ref, stage_ref, out_sems = refs
    last = outer_chunk(links_ref, upper_hbm, (a, b, c), vector_ref, left_ref, hop_ref, sems)
    quarter = last.shape[1] // 2
    low = iota(last.shape, 1) < quarter
    second = second_ref[...]
    real = [first_ref[0], jnp.where(low, second, pltpu.roll(last, quarter, 1))]
    imag = [first_ref[1], jnp.where(low, pltpu.roll(second, quarter, 1), last)]
    store_table(
        table_ref, fold_ref, jnp.concatenate(real, 1), jnp.concatenate(imag, 1), slots
    )

    def emit(n, d, packed):
        stage_ref[place_of(n, where_ref[0], near, far)] = packed.astype(BF16)

    pick_tiles(emit, owner_ref, [table_ref[...].astype(BF16)], chosen_ref, slots)
    leaving = [
        pltpu.make_async_copy(stage_ref.at[pl.ds(k * far, far)], sent_hbm[k], out_sems.at[k])
        for k in range(near)
    ]
    for copy in leaving:
        copy.start()
    wait_all(leaving)


def near_sum_kernel(where_ref, *refs):
    far = refs[0].shape[0]
    sources, outs = refs[:-far], refs[-far:]
    near = len(sources) // 2
    here = where_ref[0] // near

    def total(arrays, block):
        value = arrays[0][block].astype(F32)
        for array in arrays[1:]:
            value = value + array[block].astype(F32)
        return value

    for m in range(far):
        block = lax.rem(here + m, far)
        outs[m][0] = total(sources[:near], block).astype(outs[m].dtype)
        outs[m][1:] = total(sources[near:], block).astype(outs[m].dtype)


def finish_kernel(normalise, slots, *refs):
    sources, out_ref = refs[:-1], refs[-1]
    here = out_ref.shape[0]
    total = sources[0][...]
    for source in sources[1:]:
        total = total + source[...].astype(F32)
    for d in range(3):
        value = total[d]
        value = value * normalise
        for group in range(slots.groups):
            first = group * slots.per_group
            count = min(slots.per_group, here - first)
            out_ref[first : first + count, d * slots.columns : (d + 1) * slots.columns] = value[
                :count, group * slots.columns : (group + 1) * slots.columns
            ]


def params(mib):
    return pltpu.CompilerParams(vmem_limit_bytes=mib * 1024 * 1024)


def cost(flops, moved):
    return pl.CostEstimate(flops=flops, bytes_accessed=moved, transcendentals=0)


def chunks_of(modes):
    quarter = modes // 4
    return ((0, 2 * quarter), (2 * quarter, quarter), (3 * quarter, quarter))


def per_device(eigvecs, link_seed, ownership):
    modes, _, _, layers, plane = eigvecs.shape
    assert layers == 1
    devices = lax.axis_size("sx")
    here = ownership.shape[0] // devices
    depth = 3 * plane
    tiles = plane // LANES
    slots = Slots(modes, here)
    vmem = pl.BlockSpec(memory_space=pltpu.VMEM)
    smem = pl.BlockSpec(memory_space=pltpu.SMEM)
    anywhere = pl.BlockSpec(memory_space=pl.ANY)

    raw = eigvecs.transpose(0, 2, 3, 1, 4).reshape(3 * modes, 2, plane)
    route = [(i, (i - 1) % devices) for i in range(devices)]
    chunks = chunks_of(modes)
    own, upper = [], []
    for some, room in ((chunks[:1], 52), (chunks[1:], 50)):
        loaded = pl.pallas_call(
            functools.partial(load_kernel, [3 * first for first, _ in some]),
            name="load_modes",
            out_shape=[jax.ShapeDtypeStruct((3 * count, 2, plane), BF16) for _, count in some],
            in_specs=[anywhere] * (1 + len(own[-1:])),
            out_specs=[vmem] * len(some),
            scratch_shapes=[pltpu.SemaphoreType.DMA((len(some),))],
            compiler_params=params(room),
            cost_estimate=cost(0, 12 * modes * plane),
        )(raw, *own[-1:])
        for part, (_, count) in zip(loaded, some):
            part = part.reshape(count, 3, 2, plane).transpose(1, 2, 0, 3)
            own.append(part)
            upper.append(lax.ppermute(part, "sx", route))

    where = lax.axis_index("sx").reshape(1).astype(jnp.int32)
    owners = slots.arrange(slots.codes(ownership).reshape(devices, here))
    near = 1
    while near * near < devices:
        near *= 2
    far = devices // near
    assert near * far == devices
    flops = 4 * modes * modes * depth * 2
    wide = pltpu.VMEM((2 * modes, depth), BF16)
    table = (slots.LOW, slots.depth)
    fold_scratch = pltpu.VMEM((TM // 2, modes, LANES), F32)
    chosen_scratch = pltpu.VMEM((2, devices // 2 * slots.all_rows, slots.depth), BF16)

    block = (slots.rows, LANES)
    *sent_inner, links_x = pl.pallas_call(
        functools.partial(inner_kernel, slots, (near, far)),
        name="inner_directions",
        out_shape=[jax.ShapeDtypeStruct((far, 2) + block, BF16)] * near
        + [jax.ShapeDtypeStruct((18, tiles, LANES), F32)],
        in_specs=[smem, smem, vmem] + [anywhere] * 3,
        out_specs=[vmem] * (near + 1),
        scratch_shapes=[
            wide,
            wide,
            wide,
            pltpu.VMEM((3, 18, tiles, LANES), F32),
            pltpu.VMEM((2,) + table, F32),
            fold_scratch,
            chosen_scratch,
            pltpu.VMEM((devices, 2) + block, BF16),
            pltpu.SemaphoreType.DMA((3, 6)),
        ],
        compiler_params=params(40),
        cost_estimate=cost(6 * flops, 8 * 2**20),
    )(link_seed, where, owners, *own)
    sizes = [count for _, count in chunks]

    def outer_scratch(size):
        return [
            pltpu.VMEM((2 * size, depth), BF16),
            wide,
            pltpu.VMEM((2 * size, depth), BF16),
            pltpu.SemaphoreType.DMA((4, 6)),
        ]

    def outer(kernel, name, which, shape, before):
        return pl.pallas_call(
            kernel,
            name=name,
            out_shape=jax.ShapeDtypeStruct(shape, F32),
            in_specs=[vmem] + [anywhere] * (4 + len(before)),
            out_specs=vmem,
            scratch_shapes=outer_scratch(sizes[which]),
            compiler_params=params(24),
            cost_estimate=cost(2**20, 2**18),
        )(links_x, upper[which], *own, *before)

    first_x = outer(wide_kernel, "outer_first", 0, (2, modes, sizes[0]), [])
    second_x = outer(narrow_kernel, "outer_second", 1, (modes, 2 * sizes[1]), [first_x])
    sent = pl.pallas_call(
        functools.partial(last_kernel, slots, (near, far)),
        name="outer_last",
        out_shape=[jax.ShapeDtypeStruct((far,) + block, BF16)] * near,
        in_specs=[smem] + [vmem] * 4 + [anywhere] * 4,
        out_specs=[anywhere] * near,
        scratch_shapes=outer_scratch(sizes[2])
        + [
            pltpu.VMEM(table, F32),
            fold_scratch,
            chosen_scratch,
            pltpu.VMEM((devices,) + block, BF16),
            pltpu.SemaphoreType.DMA((near,)),
        ],
        compiler_params=params(24),
        cost_estimate=cost(2**20, 2**18),
    )(where, owners, first_x, second_x, links_x, upper[2], *own)

    def onward(step, array, size, inner):
        def target(i):
            index = i // inner % size
            return i + ((index + step) % size - index) * inner

        return lax.ppermute(array, "sx", [(i, target(i)) for i in range(devices)])

    gathered = [
        array if k == 0 else onward(k, array, near, 1)
        for arrays in (sent, sent_inner)
        for k, array in enumerate(arrays)
    ]
    halfway = pl.pallas_call(
        near_sum_kernel,
        name="sum_near",
        out_shape=[
            jax.ShapeDtypeStruct((3,) + block, F32 if m == 0 else BF16) for m in range(far)
        ],
        in_specs=[smem] + [vmem] * (2 * near),
        out_specs=[vmem] * far,
        compiler_params=params(8),
        cost_estimate=cost(2**20, 2**20),
    )(where, *gathered)
    arrived = [halfway[0]] + [onward(m, halfway[m], far, near) for m in range(1, far)]

    extent_x = layers * devices
    normalise = 1.0 / math.sqrt(12.0 * extent_x * plane)
    return pl.pallas_call(
        functools.partial(finish_kernel, normalise, slots),
        name="sum_far",
        out_shape=jax.ShapeDtypeStruct((here, 3 * slots.columns), F32),
        in_specs=[vmem] * far,
        out_specs=vmem,
        compiler_params=params(8),
    )(*arrived)


def solution(mesh):
    return jax.shard_map(
        per_device,
        mesh=mesh,
        in_specs=(P("cfg", None, None, "sx", None), P("cfg"), P()),
        out_specs=P(("cfg", "sx"), None),
        check_vma=False,
    )
```

profile of v0, /device:TPU:0, one launch (start us, length us, event | category | flops | bytes accessed | tf_op | source)
XLA Modules:
  0.0 62.8 jit_solution(4204249050987901426)
XLA Ops:
  0.0 1.4 %load_modes.2 = bf16[384,2,1024]{2,1,0:T(2,128)(2,1)S(1)} custom-call(bf16[768,2,1024]{2,1,0:T(2,128)(2,1)} %bitcast.40), custom_call_target="tpu_custom_call" | custom-call | bytes 3145728 | tf_op jit(solution)/shard_map/load_modes/pallas_call | solution.py:514
  1.4 0.5 copy.12
  1.9 5.5 %collective-permute-start = (bf16[3,2,128,1024]{3,2,1,0:T(8,128)(2,1)S(1)}, bf16[3,2,128,1024]{3,2,1,0:T(8,128)(2,1)}, u32[]{:S(2)}, u32[]{:S(2)}) collective-permute-start(bf16[3,2,128,1024]{3,2,1,0:T(8,128)(2,1)S(1)} %bitcast.19), channel_id=1, source_target_pairs={{0,15},{1,0},{2,1},{3,2},{4,3},{5,4},{6,5},{7,6},{8,7},{9,8},{10,9... | collective-permute-start | bytes 4718600 | tf_op jit(solution)/shard_map/ppermute | solution.py:527
  7.4 1.4 %load_modes.3 = (bf16[192,2,1024]{2,1,0:T(2,128)(2,1)S(1)}, bf16[192,2,1024]{2,1,0:T(2,128)(2,1)S(1)}) custom-call(bf16[768,2,1024]{2,1,0:T(2,128)(2,1)} %bitcast.41, bf16[3,2,128,1024]{3,2,1,0:T(8,128)(2,1)S(1)} %bitcast.20), custom_call_target="tpu_custom_call" | custom-call | bytes 3145728 | tf_op jit(solution)/shard_map/load_modes/pallas_call | solution.py:514
  8.8 0.2 copy.14
  9.0 0.7 %collective-permute-start.1 = (bf16[3,2,64,1024]{3,2,1,0:T(8,128)(2,1)S(1)}, bf16[3,2,64,1024]{3,2,1,0:T(8,128)(2,1)}, u32[]{:S(2)}, u32[]{:S(2)}) collective-permute-start(bf16[3,2,64,1024]{3,2,1,0:T(8,128)(2,1)S(1)} %bitcast.25), channel_id=1, source_target_pairs={{0,15},{1,0},{2,1},{3,2},{4,3},{5,4},{6,5},{7,6},{8,7},{9,8},{10,9... | collective-permute-start | bytes 2359304 | tf_op jit(solution)/shard_map/ppermute | solution.py:527
  9.7 0.2 copy.13
  10.0 0.1 collective-permute-start.2
  10.0 0.1 fusion.11
  10.1 0.1 reshape.25
  10.2 0.1 reshape.26
  10.3 0.1 copy.8
  10.5 21.8 %inner_directions.1 = (bf16[4,2,40,128]{3,2,1,0:T(8,128)(2,1)S(1)}, bf16[4,2,40,128]{3,2,1,0:T(8,128)(2,1)S(1)}, bf16[4,2,40,128]{3,2,1,0:T(8,128)(2,1)S(1)}, bf...) custom-call(s32[3]{0:T(128)S(1)} %copy-done, s32[1]{0:T(128)} %bitcast.where_ref, s32[160,16]{1,0:T(8,128)S(1)} %bitcast.38, ...), custom_call_target="tpu_custom_call" | custom-call | flops 9663676416 | bytes 8388608 | tf_op jit(solution)/shard_map/inner_directions/pallas_call | solution.py:543
  32.3 0.7 %collective-permute-start.6 = (bf16[4,2,40,128]{3,2,1,0:T(8,128)(2,1)S(1)}, bf16[4,2,40,128]{3,2,1,0:T(8,128)(2,1)S(1)}, u32[]{:S(2)}, u32[]{:S(2)}) collective-permute-start(bf16[4,2,40,128]{3,2,1,0:T(8,128)(2,1)S(1)} %get-tuple-element.28), channel_id=1, source_target_pairs={{0,1},{1,2},{2,3},{3,0},{4,5},{5,6},{6,7},{7,4},{8,9},{9,10},{10,1... | collective-permute-start | bytes 245768 | tf_op jit(solution)/shard_map/ppermute | solution.py:611
  33.0 1.0 %collective-permute-start.7 = (bf16[4,2,40,128]{3,2,1,0:T(8,128)(2,1)S(1)}, bf16[4,2,40,128]{3,2,1,0:T(8,128)(2,1)S(1)}, u32[]{:S(2)}, u32[]{:S(2)}) collective-permute-start(bf16[4,2,40,128]{3,2,1,0:T(8,128)(2,1)S(1)} %get-tuple-element.29), channel_id=1, source_target_pairs={{0,2},{1,3},{2,0},{3,1},{4,6},{5,7},{6,4},{7,5},{8,10},{9,11},{10,... | collective-permute-start | bytes 245768 | tf_op jit(solution)/shard_map/ppermute | solution.py:611
  34.0 1.4 %collective-permute-start.8 = (bf16[4,2,40,128]{3,2,1,0:T(8,128)(2,1)S(1)}, bf16[4,2,40,128]{3,2,1,0:T(8,128)(2,1)S(1)}, u32[]{:S(2)}, u32[]{:S(2)}) collective-permute-start(bf16[4,2,40,128]{3,2,1,0:T(8,128)(2,1)S(1)} %get-tuple-element.30), channel_id=1, source_target_pairs={{0,3},{1,0},{2,1},{3,2},{4,7},{5,4},{6,5},{7,6},{8,11},{9,8},{10,9... | collective-permute-start | bytes 245768 | tf_op jit(solution)/shard_map/ppermute | solution.py:611
  35.4 4.4 %outer_first.1.before_hbm.first_ref = f32[2,256,128]{2,1,0:T(8,128)S(1)} custom-call(f32[18,8,128]{2,1,0:T(8,128)S(1)} %get-tuple-element.22.links_ref, bf16[3,2,128,1024]{3,2,1,0:T(8,128)(2,1)} %collective-permute-done.upper_hbm, bf16[3,2,128,1024]{3,2,1,0:T(8,128)(2,1)S(1)} %bitcast.22, bf16[3,2,64,1024]{3,2,1,0:T(8,128)(2,1)S(1)} %bitcast.27, ...), custom_call_target="tpu_custom_call" | custom-call | flops 1048576 | bytes 262144 | tf_op jit(solution)/shard_map/outer_first/pallas_call | solution.py:575
  39.8 3.4 %outer_second.1.second_ref = f32[256,128]{1,0:T(8,128)S(1)} custom-call(f32[18,8,128]{2,1,0:T(8,128)S(1)} %get-tuple-element.22.links_ref, bf16[3,2,64,1024]{3,2,1,0:T(8,128)(2,1)} %collective-permute-done.1.upper_hbm, bf16[3,2,128,1024]{3,2,1,0:T(8,128)(2,1)S(1)} %bitcast.23, bf16[3,2,64,1024]{3,2,1,0:T(8,128)(2,1)S(1)} %bitcast.28, ...), custom_call_target="tpu_custom_call" | custom-call | flops 1048576 | bytes 262144 | tf_op jit(solution)/shard_map/outer_second/pallas_call | solution.py:575
  43.2 5.9 %outer_last.1 = (bf16[4,40,128]{2,1,0:T(8,128)(2,1)S(1)}, bf16[4,40,128]{2,1,0:T(8,128)(2,1)S(1)}, bf16[4,40,128]{2,1,0:T(8,128)(2,1)S(1)}, bf16[4,40,128]{2,1,0:T(8,128)(2,1)S(1)}) custom-call(s32[1]{0:T(128)} %bitcast.where_ref, s32[160,16]{1,0:T(8,128)S(1)} %bitcast.39, f32[2,256,128]{2,1,0:T(8,128)S(1)} %outer_first.1.before_hbm.first_ref, ...), custom_call_target="tpu_custom_call" | custom-call | flops 1048576 | bytes 262144 | tf_op jit(solution)/shard_map/outer_last/pallas_call | solution.py:588
  49.1 0.1 collective-permute-start.3
  49.2 0.7 %collective-permute-start.4 = (bf16[4,40,128]{2,1,0:T(8,128)(2,1)S(1)}, bf16[4,40,128]{2,1,0:T(8,128)(2,1)S(1)}, u32[]{:S(2)}, u32[]{:S(2)}) collective-permute-start(bf16[4,40,128]{2,1,0:T(8,128)(2,1)S(1)} %get-tuple-element.25), channel_id=1, source_target_pairs={{0,2},{1,3},{2,0},{3,1},{4,6},{5,7},{6,4},{7,5},{8,10},{9,11},{10,... | collective-permute-start | bytes 122888 | tf_op jit(solution)/shard_map/ppermute | solution.py:611
  49.8 1.4 %collective-permute-start.5 = (bf16[4,40,128]{2,1,0:T(8,128)(2,1)S(1)}, bf16[4,40,128]{2,1,0:T(8,128)(2,1)S(1)}, u32[]{:S(2)}, u32[]{:S(2)}) collective-permute-start(bf16[4,40,128]{2,1,0:T(8,128)(2,1)S(1)} %get-tuple-element.26), channel_id=1, source_target_pairs={{0,3},{1,0},{2,1},{3,2},{4,7},{5,4},{6,5},{7,6},{8,11},{9,8},{10,9... | collective-permute-start | bytes 122888 | tf_op jit(solution)/shard_map/ppermute | solution.py:611
  51.2 1.4 %collective-permute-done.3.refs_1_ = bf16[4,40,128]{2,1,0:T(8,128)(2,1)S(1)} collective-permute-done((bf16[4,40,128]{2,1,0:T(8,128)(2,1)S(1)}, bf16[4,40,128]{2,1,0:T(8,128)(2,1)S(1)}, u32[]{:S(2)}, u32[]{:S(2)}) %collective-permute-start.3) | collective-permute-done | bytes 40992 | tf_op jit(solution)/shard_map/ppermute | solution.py:611
  52.6 0.9 %collective-permute-done.4.refs_2_ = bf16[4,40,128]{2,1,0:T(8,128)(2,1)S(1)} collective-permute-done((bf16[4,40,128]{2,1,0:T(8,128)(2,1)S(1)}, bf16[4,40,128]{2,1,0:T(8,128)(2,1)S(1)}, u32[]{:S(2)}, u32[]{:S(2)}) %collective-permute-start.4) | collective-permute-done | bytes 40992 | tf_op jit(solution)/shard_map/ppermute | solution.py:611
  53.5 0.1 sum_near.1
  53.6 1.0 %collective-permute-start.10 = (bf16[3,40,128]{2,1,0:T(8,128)(2,1)S(1)}, bf16[3,40,128]{2,1,0:T(8,128)(2,1)S(1)}, u32[]{:S(2)}, u32[]{:S(2)}) collective-permute-start(bf16[3,40,128]{2,1,0:T(8,128)(2,1)S(1)} %get-tuple-element.33), channel_id=1, source_target_pairs={{0,8},{1,9},{2,10},{3,11},{4,12},{5,13},{6,14},{7,15},{8,0},{9,1},... | collective-permute-start | bytes 92168 | tf_op jit(solution)/shard_map/ppermute | solution.py:611
  54.5 1.7 %collective-permute-start.11 = (bf16[3,40,128]{2,1,0:T(8,128)(2,1)S(1)}, bf16[3,40,128]{2,1,0:T(8,128)(2,1)S(1)}, u32[]{:S(2)}, u32[]{:S(2)}) collective-permute-start(bf16[3,40,128]{2,1,0:T(8,128)(2,1)S(1)} %get-tuple-element.34), channel_id=1, source_target_pairs={{0,12},{1,13},{2,14},{3,15},{4,0},{5,1},{6,2},{7,3},{8,4},{9,5},{1... | collective-permute-start | bytes 92168 | tf_op jit(solution)/shard_map/ppermute | solution.py:611
  56.3 0.5 collective-permute-start.9
  56.8 2.4 %collective-permute-done.10.refs_2_ = bf16[3,40,128]{2,1,0:T(8,128)(2,1)S(1)} collective-permute-done((bf16[3,40,128]{2,1,0:T(8,128)(2,1)S(1)}, bf16[3,40,128]{2,1,0:T(8,128)(2,1)S(1)}, u32[]{:S(2)}, u32[]{:S(2)}) %collective-permute-start.10) | collective-permute-done | bytes 30752 | tf_op jit(solution)/shard_map/ppermute | solution.py:611
  59.2 0.2 collective-permute-done.11.refs_3_
  59.4 2.7 %collective-permute-done.9.refs_1_ = bf16[3,40,128]{2,1,0:T(8,128)(2,1)S(1)} collective-permute-done((bf16[3,40,128]{2,1,0:T(8,128)(2,1)S(1)}, bf16[3,40,128]{2,1,0:T(8,128)(2,1)S(1)}, u32[]{:S(2)}, u32[]{:S(2)}) %collective-permute-start.9) | collective-permute-done | bytes 30752 | tf_op jit(solution)/shard_map/ppermute | solution.py:611
  62.1 0.8 %sum_far.1 = f32[130,96]{1,0:T(8,128)} custom-call(f32[3,40,128]{2,1,0:T(8,128)S(1)} %get-tuple-element.31.refs_0_, bf16[3,40,128]{2,1,0:T(8,128)(2,1)S(1)} %collective-permute-done.9.refs_1_, bf16[3,40,128]{2,1,0:T(8,128)(2,1)S(1)} %collective-permute-done.10.refs_2_, bf16[3,40,128]{2,1,0:T(8,128)(2,1)S(1)} %collective-permute-done.11.refs_3_), custom_call_target="tpu_custom_call" | custom-call | tf_op jit(solution)/shard_map/sum_far/pallas_call | solution.py:633
  (13 shorter events, 0.1 us)
Async XLA Ops:
  1.9 32.2 %collective-permute-start = (bf16[3,2,128,1024]{3,2,1,0:T(8,128)(2,1)S(1)}, bf16[3,2,128,1024]{3,2,1,0:T(8,128)(2,1)}, u32[]{:S(2)}, u32[]{:S(2)}) collective-permute-start(bf16[3,2,128,1024]{3,2,1,0:T(8,128)(2,1)S(1)} %bitcast.19), channel_id=1, source_target_pairs={{0,15},{1,0},{2,1},{3,2},{4,3},{5,4},{6,5},{7,6},{8,7},{9,8},{10,9... | collective-permute-start | bytes 4718600 | tf_op jit(solution)/shard_map/ppermute | solution.py:527
  8.8 1.3 %copy-start.1 = (s32[2080]{0:T(1024)S(1)}, s32[2080]{0:T(1024)}, u32[]{:S(2)}) copy-start(s32[2080]{0:T(1024)} %param.5) | copy-start | bytes 24964
  8.8 1.7 %copy-start = (s32[3]{0:T(128)S(1)}, s32[3]{0:T(128)}, u32[]{:S(2)}) copy-start(s32[3]{0:T(128)} %seed_ref.1) | copy-start | bytes 40
  9.0 30.8 %collective-permute-start.1 = (bf16[3,2,64,1024]{3,2,1,0:T(8,128)(2,1)S(1)}, bf16[3,2,64,1024]{3,2,1,0:T(8,128)(2,1)}, u32[]{:S(2)}, u32[]{:S(2)}) collective-permute-start(bf16[3,2,64,1024]{3,2,1,0:T(8,128)(2,1)S(1)} %bitcast.25), channel_id=1, source_target_pairs={{0,15},{1,0},{2,1},{3,2},{4,3},{5,4},{6,5},{7,6},{8,7},{9,8},{10,9... | collective-permute-start | bytes 2359304 | tf_op jit(solution)/shard_map/ppermute | solution.py:527
  10.0 33.3 %collective-permute-start.2 = (bf16[3,2,64,1024]{3,2,1,0:T(8,128)(2,1)S(1)}, bf16[3,2,64,1024]{3,2,1,0:T(8,128)(2,1)}, u32[]{:S(2)}, u32[]{:S(2)}) collective-permute-start(bf16[3,2,64,1024]{3,2,1,0:T(8,128)(2,1)S(1)} %bitcast.30), channel_id=1, source_target_pairs={{0,15},{1,0},{2,1},{3,2},{4,3},{5,4},{6,5},{7,6},{8,7},{9,8},{10,9... | collective-permute-start | bytes 2359304 | tf_op jit(solution)/shard_map/ppermute | solution.py:527
  32.3 17.6 %collective-permute-start.6 = (bf16[4,2,40,128]{3,2,1,0:T(8,128)(2,1)S(1)}, bf16[4,2,40,128]{3,2,1,0:T(8,128)(2,1)S(1)}, u32[]{:S(2)}, u32[]{:S(2)}) collective-permute-start(bf16[4,2,40,128]{3,2,1,0:T(8,128)(2,1)S(1)} %get-tuple-element.28), channel_id=1, source_target_pairs={{0,1},{1,2},{2,3},{3,0},{4,5},{5,6},{6,7},{7,4},{8,9},{9,10},{10,1... | collective-permute-start | bytes 245768 | tf_op jit(solution)/shard_map/ppermute | solution.py:611
  33.0 18.2 %collective-permute-start.7 = (bf16[4,2,40,128]{3,2,1,0:T(8,128)(2,1)S(1)}, bf16[4,2,40,128]{3,2,1,0:T(8,128)(2,1)S(1)}, u32[]{:S(2)}, u32[]{:S(2)}) collective-permute-start(bf16[4,2,40,128]{3,2,1,0:T(8,128)(2,1)S(1)} %get-tuple-element.29), channel_id=1, source_target_pairs={{0,2},{1,3},{2,0},{3,1},{4,6},{5,7},{6,4},{7,5},{8,10},{9,11},{10,... | collective-permute-start | bytes 245768 | tf_op jit(solution)/shard_map/ppermute | solution.py:611
  34.0 17.2 %collective-permute-start.8 = (bf16[4,2,40,128]{3,2,1,0:T(8,128)(2,1)S(1)}, bf16[4,2,40,128]{3,2,1,0:T(8,128)(2,1)S(1)}, u32[]{:S(2)}, u32[]{:S(2)}) collective-permute-start(bf16[4,2,40,128]{3,2,1,0:T(8,128)(2,1)S(1)} %get-tuple-element.30), channel_id=1, source_target_pairs={{0,3},{1,0},{2,1},{3,2},{4,7},{5,4},{6,5},{7,6},{8,11},{9,8},{10,9... | collective-permute-start | bytes 245768 | tf_op jit(solution)/shard_map/ppermute | solution.py:611
  49.1 3.5 %collective-permute-start.3 = (bf16[4,40,128]{2,1,0:T(8,128)(2,1)S(1)}, bf16[4,40,128]{2,1,0:T(8,128)(2,1)S(1)}, u32[]{:S(2)}, u32[]{:S(2)}) collective-permute-start(bf16[4,40,128]{2,1,0:T(8,128)(2,1)S(1)} %get-tuple-element.24), channel_id=1, source_target_pairs={{0,1},{1,2},{2,3},{3,0},{4,5},{5,6},{6,7},{7,4},{8,9},{9,10},{10,1... | collective-permute-start | bytes 122888 | tf_op jit(solution)/shard_map/ppermute | solution.py:611
  49.2 4.3 %collective-permute-start.4 = (bf16[4,40,128]{2,1,0:T(8,128)(2,1)S(1)}, bf16[4,40,128]{2,1,0:T(8,128)(2,1)S(1)}, u32[]{:S(2)}, u32[]{:S(2)}) collective-permute-start(bf16[4,40,128]{2,1,0:T(8,128)(2,1)S(1)} %get-tuple-element.25), channel_id=1, source_target_pairs={{0,2},{1,3},{2,0},{3,1},{4,6},{5,7},{6,4},{7,5},{8,10},{9,11},{10,... | collective-permute-start | bytes 122888 | tf_op jit(solution)/shard_map/ppermute | solution.py:611
  49.8 3.6 %collective-permute-start.5 = (bf16[4,40,128]{2,1,0:T(8,128)(2,1)S(1)}, bf16[4,40,128]{2,1,0:T(8,128)(2,1)S(1)}, u32[]{:S(2)}, u32[]{:S(2)}) collective-permute-start(bf16[4,40,128]{2,1,0:T(8,128)(2,1)S(1)} %get-tuple-element.26), channel_id=1, source_target_pairs={{0,3},{1,0},{2,1},{3,2},{4,7},{5,4},{6,5},{7,6},{8,11},{9,8},{10,9... | collective-permute-start | bytes 122888 | tf_op jit(solution)/shard_map/ppermute | solution.py:611
  53.6 5.6 %collective-permute-start.10 = (bf16[3,40,128]{2,1,0:T(8,128)(2,1)S(1)}, bf16[3,40,128]{2,1,0:T(8,128)(2,1)S(1)}, u32[]{:S(2)}, u32[]{:S(2)}) collective-permute-start(bf16[3,40,128]{2,1,0:T(8,128)(2,1)S(1)} %get-tuple-element.33), channel_id=1, source_target_pairs={{0,8},{1,9},{2,10},{3,11},{4,12},{5,13},{6,14},{7,15},{8,0},{9,1},... | collective-permute-start | bytes 92168 | tf_op jit(solution)/shard_map/ppermute | solution.py:611
  54.5 4.9 %collective-permute-start.11 = (bf16[3,40,128]{2,1,0:T(8,128)(2,1)S(1)}, bf16[3,40,128]{2,1,0:T(8,128)(2,1)S(1)}, u32[]{:S(2)}, u32[]{:S(2)}) collective-permute-start(bf16[3,40,128]{2,1,0:T(8,128)(2,1)S(1)} %get-tuple-element.34), channel_id=1, source_target_pairs={{0,12},{1,13},{2,14},{3,15},{4,0},{5,1},{6,2},{7,3},{8,4},{9,5},{1... | collective-permute-start | bytes 92168 | tf_op jit(solution)/shard_map/ppermute | solution.py:611
  56.3 5.8 %collective-permute-start.9 = (bf16[3,40,128]{2,1,0:T(8,128)(2,1)S(1)}, bf16[3,40,128]{2,1,0:T(8,128)(2,1)S(1)}, u32[]{:S(2)}, u32[]{:S(2)}) collective-permute-start(bf16[3,40,128]{2,1,0:T(8,128)(2,1)S(1)} %get-tuple-element.32), channel_id=1, source_target_pairs={{0,4},{1,5},{2,6},{3,7},{4,8},{5,9},{6,10},{7,11},{8,12},{9,13},{1... | collective-permute-start | bytes 92168 | tf_op jit(solution)/shard_map/ppermute | solution.py:611
where the time goes:
time: 63.1 us; the launch traced here: 62.8 us
  Pallas kernels  39.1 us (62%)
  starting transfers between devices  14.8 us (23%)
  waiting for transfers between devices  7.58 us (12%)
  local copies, waits for them, and re-layouts  1.19 us (2%)
    pallas_call x1, Pallas kernels, per_device(): pl.pallas_call(functools.partial(inner_kernel, slots, (near, far)), name=...  21.8 us
    ppermute x9, starting transfers between devices, onward(): return lax.ppermute(array, 'sx', [(i, target(i)) for i in range(devices)])  8.46 us
    pallas_call x2, Pallas kernels, outer(): pl.pallas_call(kernel, name=name, out_shape=jax.ShapeDtypeStruct(shape, F...  7.77 us
    ppermute x9, waiting for transfers between devices, onward(): return lax.ppermute(array, 'sx', [(i, target(i)) for i in range(devices)])  7.57 us
    ppermute x3, starting transfers between devices, per_device(): upper.append(lax.ppermute(part, 'sx', route))  6.3 us
    pallas_call x1, Pallas kernels, per_device(): pl.pallas_call(functools.partial(last_kernel, slots, (near, far)), name='...  5.89 us
    pallas_call x2, Pallas kernels, per_device(): pl.pallas_call(functools.partial(load_kernel, [3 * first for first, _ in...  2.8 us
  transfers between devices with their start and end apart: 12, of which 5 were waited for; matrix products, arithmetic and copies ran while one was open for 1% of the time, Pallas kernels for 59%

commit v1 on v0

--- a/solution.py
+++ b/solution.py
@@ -13,6 +13,7 @@
 LANES = 128
 MODULUS = 46337
 STEP = 32
+PIECES = 4
 F32 = jnp.float32
 BF16 = jnp.bfloat16
 NT = (((1,), (1,)), ((), ()))
@@ -62,13 +63,16 @@
         [sa * cb * cg + ca * sg, -sa * cb * sg + ca * cg, sa * sb],
         [-sb * cg, sb * sg, cb],
     ]
-    left = [a[3], a[4], -a[3] - a[4]]
-    right = [a[5], a[6], -a[5] - a[6]]
+    def phases(first, second):
+        c1, s1, c2, s2 = jnp.cos(first), jnp.sin(first), jnp.cos(second), jnp.sin(second)
+        return [(c1, s1), (c2, s2), (c1 * c2 - s1 * s2, -(s1 * c2 + c1 * s2))]
+
+    left, right = phases(a[3], a[4]), phases(a[5], a[6])
     for c in range(3):
         for s in range(3):
-            phase = left[c] + right[s]
-            u_ref[2 * (3 * c + s)] = rotation[c][s] * jnp.cos(phase)
-            u_ref[2 * (3 * c + s) + 1] = rotation[c][s] * jnp.sin(phase)
+            (cl, sl), (cr, sr) = left[c], right[s]
+            u_ref[2 * (3 * c + s)] = rotation[c][s] * (cl * cr - sl * sr)
+            u_ref[2 * (3 * c + s) + 1] = rotation[c][s] * (sl * cr + cl * sr)
 
 
 def hop(vector_ref, out_ref, u_ref, first, count):
@@ -339,10 +343,17 @@
 
 def load_kernel(starts, whole_hbm, *refs):
     parts, sems = refs[-1 - len(starts) : -1], refs[-1]
-    copies = [
-        pltpu.make_async_copy(whole_hbm.at[pl.ds(start, part.shape[0])], part, sems.at[k])
-        for k, (start, part) in enumerate(zip(starts, parts))
-    ]
+    copies = []
+    for k, (start, part) in enumerate(zip(starts, parts)):
+        count = part.shape[0] // PIECES
+        for piece in range(PIECES):
+            copies.append(
+                pltpu.make_async_copy(
+                    whole_hbm.at[pl.ds(start + piece * count, count)],
+                    part.at[pl.ds(piece * count, count)],
+                    sems.at[k, piece],
+                )
+            )
     for copy in copies:
         copy.start()
     wait_all(copies)
@@ -365,13 +376,15 @@
 ):
     near, far = grid
     sent, refs = refs[:near], refs[near:]
-    links_x_ref, vector_ref, left_ref, hop_ref, links_ref, *refs = refs
-    table_ref, fold_ref, chosen_ref, stage_ref, sems = refs
+    links_x_ref, own_hbm, vector_ref, left_ref, hop_ref, links_ref, *refs = refs
+    table_ref, fold_ref, chosen_ref, stage_ref, sems, own_sem = refs
     modes, plane = vector_ref.shape[0] // 2, vector_ref.shape[1] // 3
     copies = load_all((a, b, c), vector_ref, sems)
     store_all_links(links_ref, seed_ref, where_ref[0])
     links_x_ref[...] = links_ref[0]
     wait_all(copies)
+    own = pltpu.make_async_copy(vector_ref, own_hbm, own_sem)
+    own.start()
     tables = []
     for d, store_left in ((1, store_left_y), (2, store_left_z)):
         store_left(left_ref, vector_ref, plane)
@@ -386,24 +399,35 @@
     pick_tiles(emit, owner_ref, [t[...].astype(BF16) for t in tables], chosen_ref, slots)
     for k in range(near):
         sent[k][...] = stage_ref[k * far : (k + 1) * far]
+    own.wait()
 
 
 def outer_chunk(links_ref, upper_hbm, own_hbm, vector_ref, left_ref, hop_ref, sems):
-    arriving = load_modes(upper_hbm, vector_ref, sems.at[3], 0)
-    own = load_all(own_hbm, left_ref, sems)
+    arriving = load_modes(upper_hbm, vector_ref, sems.at[0], 0)
+    count = left_ref.shape[0] // PIECES
+    own = [
+        pltpu.make_async_copy(
+            own_hbm.at[pl.ds(piece * count, count)],
+            left_ref.at[pl.ds(piece * count, count)],
+            sems.at[1, piece],
+        )
+        for piece in range(PIECES)
+    ]
+    for copy in own:
+        copy.start()
     wait_all(arriving)
     hop(vector_ref, hop_ref, links_ref, 0, vector_ref.shape[0] // 2)
     wait_all(own)
     return products(left_ref, hop_ref)
 
 
-def wide_kernel(links_ref, upper_hbm, a, b, c, out_ref, *scratch):
-    out_ref[0], out_ref[1] = outer_chunk(links_ref, upper_hbm, (a, b, c), *scratch)
-
-
-def narrow_kernel(links_ref, upper_hbm, a, b, c, before_hbm, out_ref, *scratch):
+def wide_kernel(links_ref, upper_hbm, own_hbm, out_ref, *scratch):
+    out_ref[0], out_ref[1] = outer_chunk(links_ref, upper_hbm, own_hbm, *scratch)
+
+
+def narrow_kernel(links_ref, upper_hbm, own_hbm, before_hbm, out_ref, *scratch):
     del before_hbm
-    out_ref[...] = outer_chunk(links_ref, upper_hbm, (a, b, c), *scratch)
+    out_ref[...] = outer_chunk(links_ref, upper_hbm, own_hbm, *scratch)
 
 
 def last_kernel(
@@ -415,15 +439,13 @@
     second_ref,
     links_ref,
     upper_hbm,
-    a,
-    b,
-    c,
+    own_hbm,
     *refs,
 ):
     near, far = grid
     sent_hbm, refs = refs[:near], refs[near:]
     vector_ref, left_ref, hop_ref, sems, table_ref, fold_ref, chosen_ref, stage_ref, out_sems = refs
-    last = outer_chunk(links_ref, upper_hbm, (a, b, c), vector_ref, left_ref, hop_ref, sems)
+    last = outer_chunk(links_ref, upper_hbm, own_hbm, vector_ref, left_ref, hop_ref, sems)
     quarter = last.shape[1] // 2
     low = iota(last.shape, 1) < quarter
     second = second_ref[...]
@@ -517,7 +539,7 @@
             out_shape=[jax.ShapeDtypeStruct((3 * count, 2, plane), BF16) for _, count in some],
             in_specs=[anywhere] * (1 + len(own[-1:])),
             out_specs=[vmem] * len(some),
-            scratch_shapes=[pltpu.SemaphoreType.DMA((len(some),))],
+            scratch_shapes=[pltpu.SemaphoreType.DMA((len(some), PIECES))],
             compiler_params=params(room),
             cost_estimate=cost(0, 12 * modes * plane),
         )(raw, *own[-1:])
@@ -540,13 +562,16 @@
     chosen_scratch = pltpu.VMEM((2, devices // 2 * slots.all_rows, slots.depth), BF16)
 
     block = (slots.rows, LANES)
-    *sent_inner, links_x = pl.pallas_call(
+    *sent_inner, links_x, left = pl.pallas_call(
         functools.partial(inner_kernel, slots, (near, far)),
         name="inner_directions",
         out_shape=[jax.ShapeDtypeStruct((far, 2) + block, BF16)] * near
-        + [jax.ShapeDtypeStruct((18, tiles, LANES), F32)],
+        + [
+            jax.ShapeDtypeStruct((18, tiles, LANES), F32),
+            jax.ShapeDtypeStruct((2 * modes, depth), BF16),
+        ],
         in_specs=[smem, smem, vmem] + [anywhere] * 3,
-        out_specs=[vmem] * (near + 1),
+        out_specs=[vmem] * (near + 1) + [anywhere],
         scratch_shapes=[
             wide,
             wide,
@@ -557,6 +582,7 @@
             chosen_scratch,
             pltpu.VMEM((devices, 2) + block, BF16),
             pltpu.SemaphoreType.DMA((3, 6)),
+            pltpu.SemaphoreType.DMA,
         ],
         compiler_params=params(40),
         cost_estimate=cost(6 * flops, 8 * 2**20),
@@ -568,7 +594,7 @@
             pltpu.VMEM((2 * size, depth), BF16),
             wide,
             pltpu.VMEM((2 * size, depth), BF16),
-            pltpu.SemaphoreType.DMA((4, 6)),
+            pltpu.SemaphoreType.DMA((2, 6)),
         ]
 
     def outer(kernel, name, which, shape, before):
@@ -576,12 +602,12 @@
             kernel,
             name=name,
             out_shape=jax.ShapeDtypeStruct(shape, F32),
-            in_specs=[vmem] + [anywhere] * (4 + len(before)),
+            in_specs=[vmem] + [anywhere] * (2 + len(before)),
             out_specs=vmem,
             scratch_shapes=outer_scratch(sizes[which]),
             compiler_params=params(24),
             cost_estimate=cost(2**20, 2**18),
-        )(links_x, upper[which], *own, *before)
+        )(links_x, upper[which], left, *before)
 
     first_x = outer(wide_kernel, "outer_first", 0, (2, modes, sizes[0]), [])
     second_x = outer(narrow_kernel, "outer_second", 1, (modes, 2 * sizes[1]), [first_x])
@@ -589,7 +615,7 @@
         functools.partial(last_kernel, slots, (near, far)),
         name="outer_last",
         out_shape=[jax.ShapeDtypeStruct((far,) + block, BF16)] * near,
-        in_specs=[smem] + [vmem] * 4 + [anywhere] * 4,
+        in_specs=[smem] + [vmem] * 4 + [anywhere] * 2,
         out_specs=[anywhere] * near,
         scratch_shapes=outer_scratch(sizes[2])
         + [
@@ -601,7 +627,7 @@
         ],
         compiler_params=params(24),
         cost_estimate=cost(2**20, 2**18),
-    )(where, owners, first_x, second_x, links_x, upper[2], *own)
+    )(where, owners, first_x, second_x, links_x, upper[2], left)
 
     def onward(step, array, size, inner):
         def target(i):

time: 63.1 us -> 62.9 us (level)
  local copies, waits for them, and re-layouts: 1.19 us -> 3.02 us
  starting transfers between devices: 14.8 us -> 13.6 us
    reshape x3, local copies, waits for them, and re-layouts: 0.87 us -> 2.7 us  [per_device(): part = part.reshape(count, 3, 2, plane).transpose(1, 2, 0, 3)]
    pallas_call x2, Pallas kernels: 7.77 us -> 6.53 us  [outer(): pl.pallas_call(kernel, name=name, out_shape=jax.ShapeDtypeStruct(shape, F...]
    ppermute x9, starting transfers between devices: 8.46 us -> 7.38 us  [onward(): return lax.ppermute(array, 'sx', [(i, target(i)) for i in range(devices)])]
  transfers between devices with their start and end apart: 12 -> 12, of which waited for: 5 -> 4; matrix products, arithmetic and copies ran while one was open for 1% -> 4% of each run, Pallas kernels for 59% -> 58%
where the time goes in v1:
time: 62.9 us; the launch traced here: 62.7 us
  Pallas kernels  38.5 us (61%)
  starting transfers between devices  13.6 us (22%)
  waiting for transfers between devices  7.43 us (12%)
  local copies, waits for them, and re-layouts  3.02 us (5%)
    pallas_call x1, Pallas kernels, per_device(): pl.pallas_call(functools.partial(inner_kernel, slots, (near, far)), name=...  22.4 us
    ppermute x9, waiting for transfers between devices, onward(): return lax.ppermute(array, 'sx', [(i, target(i)) for i in range(devices)])  7.42 us
    ppermute x9, starting transfers between devices, onward(): return lax.ppermute(array, 'sx', [(i, target(i)) for i in range(devices)])  7.38 us
    pallas_call x2, Pallas kernels, outer(): pl.pallas_call(kernel, name=name, out_shape=jax.ShapeDtypeStruct(shape, F...  6.53 us
    ppermute x3, starting transfers between devices, per_device(): upper.append(lax.ppermute(part, 'sx', route))  6.19 us
    pallas_call x1, Pallas kernels, per_device(): pl.pallas_call(functools.partial(last_kernel, slots, (near, far)), name='...  5.78 us
    pallas_call x2, Pallas kernels, per_device(): pl.pallas_call(functools.partial(load_kernel, [3 * first for first, _ in...  2.91 us
    reshape x3, local copies, waits for them, and re-layouts, per_device(): part = part.reshape(count, 3, 2, plane).transpose(1, 2, 0, 3)  2.7 us
  transfers between devices with their start and end apart: 12, of which 4 were waited for; matrix products, arithmetic and copies ran while one was open for 4% of the time, Pallas kernels for 58%

profile of v1, /device:TPU:0, one launch (start us, length us, event | category | flops | bytes accessed | tf_op | source)
XLA Modules:
  0.0 62.7 jit_solution(2705471673563965375)
XLA Ops:
  0.0 1.4 %load_modes.2 = bf16[384,2,1024]{2,1,0:T(2,128)(2,1)S(1)} custom-call(bf16[768,2,1024]{2,1,0:T(2,128)(2,1)} %bitcast.27), custom_call_target="tpu_custom_call" | custom-call | bytes 3145728 | tf_op jit(solution)/shard_map/load_modes/pallas_call | solution.py:536
  1.4 0.5 copy.12
  1.9 5.5 %collective-permute-start = (bf16[3,2,128,1024]{3,2,1,0:T(8,128)(2,1)S(1)}, bf16[3,2,128,1024]{3,2,1,0:T(8,128)(2,1)S(1)}, u32[]{:S(2)}, u32[]{:S(2)}) collective-permute-start(bf16[3,2,128,1024]{3,2,1,0:T(8,128)(2,1)S(1)} %bitcast.19), channel_id=1, source_target_pairs={{0,15},{1,0},{2,1},{3,2},{4,3},{5,4},{6,5},{7,6},{8,7},{9,8},{10,9... | collective-permute-start | bytes 4718600 | tf_op jit(solution)/shard_map/ppermute | solution.py:549
  7.3 1.5 %load_modes.3 = (bf16[192,2,1024]{2,1,0:T(2,128)(2,1)S(1)}, bf16[192,2,1024]{2,1,0:T(2,128)(2,1)S(1)}) custom-call(bf16[768,2,1024]{2,1,0:T(2,128)(2,1)} %bitcast.28, bf16[3,2,128,1024]{3,2,1,0:T(8,128)(2,1)S(1)} %bitcast.20), custom_call_target="tpu_custom_call" | custom-call | bytes 3145728 | tf_op jit(solution)/shard_map/load_modes/pallas_call | solution.py:536
  8.9 0.0 copy-start.1
  8.9 1.1 %copy.14 = bf16[64,3,2,1024]{3,0,2,1:T(8,128)(2,1)} copy(bf16[64,3,2,1024]{3,2,1,0:T(2,128)(2,1)S(1)} %bitcast.24) | data formatting | bytes 1572864 | tf_op jit(solution)/shard_map/reshape | solution.py:547
  10.0 0.7 %collective-permute-start.1 = (bf16[3,2,64,1024]{3,2,1,0:T(8,128)(2,1)}, bf16[3,2,64,1024]{3,2,1,0:T(8,128)(2,1)}, u32[]{:S(2)}, u32[]{:S(2)}) collective-permute-start(bf16[3,2,64,1024]{3,2,1,0:T(8,128)(2,1)} %bitcast.18.b), channel_id=1, source_target_pairs={{0,15},{1,0},{2,1},{3,2},{4,3},{5,4},{6,5},{7,6},{8,7},{9,8},{10,9... | collective-permute-start | bytes 2359304 | tf_op jit(solution)/shard_map/ppermute | solution.py:549
  10.7 1.1 %copy.13 = bf16[64,3,2,1024]{3,0,2,1:T(8,128)(2,1)} copy(bf16[64,3,2,1024]{3,2,1,0:T(2,128)(2,1)S(1)} %bitcast.23) | data formatting | bytes 1572864 | tf_op jit(solution)/shard_map/reshape | solution.py:547
  11.8 0.0 collective-permute-start.2
  11.9 0.1 fusion.11
  11.9 0.1 reshape.25
  12.0 0.1 reshape.26
  12.1 0.1 copy.8
  12.3 22.4 %inner_directions.1 = (bf16[4,2,40,128]{3,2,1,0:T(8,128)(2,1)S(1)}, bf16[4,2,40,128]{3,2,1,0:T(8,128)(2,1)S(1)}, bf16[4,2,40,128]{3,2,1,0:T(8,128)(2,1)S(1)}, bf...) custom-call(s32[3]{0:T(128)S(1)} %copy-done, s32[1]{0:T(128)} %bitcast.where_ref, ...), custom_call_target="tpu_custom_call" | custom-call | flops 9663676416 | bytes 8388608 | tf_op jit(solution)/shard_map/inner_directions/pallas_call | solution.py:565
  34.7 0.7 %collective-permute-start.6 = (bf16[4,2,40,128]{3,2,1,0:T(8,128)(2,1)S(1)}, bf16[4,2,40,128]{3,2,1,0:T(8,128)(2,1)S(1)}, u32[]{:S(2)}, u32[]{:S(2)}) collective-permute-start(bf16[4,2,40,128]{3,2,1,0:T(8,128)(2,1)S(1)} %get-tuple-element.30), channel_id=1, source_target_pairs={{0,1},{1,2},{2,3},{3,0},{4,5},{5,6},{6,7},{7,4},{8,9},{9,10},{10,1... | collective-permute-start | bytes 245768 | tf_op jit(solution)/shard_map/ppermute | solution.py:637
  35.4 1.0 %collective-permute-start.7 = (bf16[4,2,40,128]{3,2,1,0:T(8,128)(2,1)S(1)}, bf16[4,2,40,128]{3,2,1,0:T(8,128)(2,1)S(1)}, u32[]{:S(2)}, u32[]{:S(2)}) collective-permute-start(bf16[4,2,40,128]{3,2,1,0:T(8,128)(2,1)S(1)} %get-tuple-element.31), channel_id=1, source_target_pairs={{0,2},{1,3},{2,0},{3,1},{4,6},{5,7},{6,4},{7,5},{8,10},{9,11},{10,... | collective-permute-start | bytes 245768 | tf_op jit(solution)/shard_map/ppermute | solution.py:637
  36.5 1.4 %collective-permute-start.8 = (bf16[4,2,40,128]{3,2,1,0:T(8,128)(2,1)S(1)}, bf16[4,2,40,128]{3,2,1,0:T(8,128)(2,1)S(1)}, u32[]{:S(2)}, u32[]{:S(2)}) collective-permute-start(bf16[4,2,40,128]{3,2,1,0:T(8,128)(2,1)S(1)} %get-tuple-element.32), channel_id=1, source_target_pairs={{0,3},{1,0},{2,1},{3,2},{4,7},{5,4},{6,5},{7,6},{8,11},{9,8},{10,9... | collective-permute-start | bytes 245768 | tf_op jit(solution)/shard_map/ppermute | solution.py:637
  37.9 3.2 %outer_first.1.before_hbm.first_ref = f32[2,256,128]{2,1,0:T(8,128)S(1)} custom-call(f32[18,8,128]{2,1,0:T(8,128)S(1)} %get-tuple-element.23.links_ref, bf16[3,2,128,1024]{3,2,1,0:T(8,128)(2,1)S(1)} %collective-permute-done.upper_hbm, bf16[512,3072]{1,0:T(8,128)(2,1)S(1)} %get-tuple-element.24.own_hbm), custom_call_target="tpu_custom_call" | custom-call | flops 1048576 | bytes 262144 | tf_op jit(solution)/shard_map/outer_first/pallas_call | solution.py:601
  41.1 3.3 %outer_second.1.second_ref = f32[256,128]{1,0:T(8,128)S(1)} custom-call(f32[18,8,128]{2,1,0:T(8,128)S(1)} %get-tuple-element.23.links_ref, bf16[3,2,64,1024]{3,2,1,0:T(8,128)(2,1)} %collective-permute-done.1.upper_hbm, bf16[512,3072]{1,0:T(8,128)(2,1)S(1)} %get-tuple-element.24.own_hbm, f32[2,256,128]{2,1,0:T(8,128)S(1)} %outer_first.1.before_hbm.first_ref), custom_call_target="tpu_custom_call" | custom-call | flops 1048576 | bytes 262144 | tf_op jit(solution)/shard_map/outer_second/pallas_call | solution.py:601
  44.4 5.8 %outer_last.1 = (bf16[4,40,128]{2,1,0:T(8,128)(2,1)S(1)}, bf16[4,40,128]{2,1,0:T(8,128)(2,1)S(1)}, bf16[4,40,128]{2,1,0:T(8,128)(2,1)S(1)}, bf16[4,40,128]{2,1,0:T(8,128)(2,1)S(1)}) custom-call(s32[1]{0:T(128)} %bitcast.where_ref, s32[160,16]{1,0:T(8,128)S(1)} %bitcast.26, f32[2,256,128]{2,1,0:T(8,128)S(1)} %outer_first.1.before_hbm.first_ref, ...), custom_call_target="tpu_custom_call" | custom-call | flops 1048576 | bytes 262144 | tf_op jit(solution)/shard_map/outer_last/pallas_call | solution.py:614
  50.2 0.1 collective-permute-start.3
  50.3 0.6 collective-permute-start.4
  50.9 1.4 %collective-permute-start.5 = (bf16[4,40,128]{2,1,0:T(8,128)(2,1)S(1)}, bf16[4,40,128]{2,1,0:T(8,128)(2,1)S(1)}, u32[]{:S(2)}, u32[]{:S(2)}) collective-permute-start(bf16[4,40,128]{2,1,0:T(8,128)(2,1)S(1)} %get-tuple-element.28), channel_id=1, source_target_pairs={{0,3},{1,0},{2,1},{3,2},{4,7},{5,4},{6,5},{7,6},{8,11},{9,8},{10,9... | collective-permute-start | bytes 122888 | tf_op jit(solution)/shard_map/ppermute | solution.py:637
  52.3 1.4 %collective-permute-done.3.refs_1_ = bf16[4,40,128]{2,1,0:T(8,128)(2,1)S(1)} collective-permute-done((bf16[4,40,128]{2,1,0:T(8,128)(2,1)S(1)}, bf16[4,40,128]{2,1,0:T(8,128)(2,1)S(1)}, u32[]{:S(2)}, u32[]{:S(2)}) %collective-permute-start.3) | collective-permute-done | bytes 40992 | tf_op jit(solution)/shard_map/ppermute | solution.py:637
  53.7 0.9 %collective-permute-done.4.refs_2_ = bf16[4,40,128]{2,1,0:T(8,128)(2,1)S(1)} collective-permute-done((bf16[4,40,128]{2,1,0:T(8,128)(2,1)S(1)}, bf16[4,40,128]{2,1,0:T(8,128)(2,1)S(1)}, u32[]{:S(2)}, u32[]{:S(2)}) %collective-permute-start.4) | collective-permute-done | bytes 40992 | tf_op jit(solution)/shard_map/ppermute | solution.py:637
  54.6 0.1 sum_near.1
  54.6 0.1 collective-permute-start.10
  54.7 1.4 %collective-permute-start.11 = (bf16[3,40,128]{2,1,0:T(8,128)(2,1)S(1)}, bf16[3,40,128]{2,1,0:T(8,128)(2,1)S(1)}, u32[]{:S(2)}, u32[]{:S(2)}) collective-permute-start(bf16[3,40,128]{2,1,0:T(8,128)(2,1)S(1)} %get-tuple-element.36), channel_id=1, source_target_pairs={{0,12},{1,13},{2,14},{3,15},{4,0},{5,1},{6,2},{7,3},{8,4},{9,5},{1... | collective-permute-start | bytes 92168 | tf_op jit(solution)/shard_map/ppermute | solution.py:637
  56.1 0.7 %collective-permute-start.9 = (bf16[3,40,128]{2,1,0:T(8,128)(2,1)S(1)}, bf16[3,40,128]{2,1,0:T(8,128)(2,1)S(1)}, u32[]{:S(2)}, u32[]{:S(2)}) collective-permute-start(bf16[3,40,128]{2,1,0:T(8,128)(2,1)S(1)} %get-tuple-element.34), channel_id=1, source_target_pairs={{0,4},{1,5},{2,6},{3,7},{4,8},{5,9},{6,10},{7,11},{8,12},{9,13},{1... | collective-permute-start | bytes 92168 | tf_op jit(solution)/shard_map/ppermute | solution.py:637
  56.8 3.0 %collective-permute-done.10.refs_2_ = bf16[3,40,128]{2,1,0:T(8,128)(2,1)S(1)} collective-permute-done((bf16[3,40,128]{2,1,0:T(8,128)(2,1)S(1)}, bf16[3,40,128]{2,1,0:T(8,128)(2,1)S(1)}, u32[]{:S(2)}, u32[]{:S(2)}) %collective-permute-start.10) | collective-permute-done | bytes 30752 | tf_op jit(solution)/shard_map/ppermute | solution.py:637
  59.8 2.1 %collective-permute-done.9.refs_1_ = bf16[3,40,128]{2,1,0:T(8,128)(2,1)S(1)} collective-permute-done((bf16[3,40,128]{2,1,0:T(8,128)(2,1)S(1)}, bf16[3,40,128]{2,1,0:T(8,128)(2,1)S(1)}, u32[]{:S(2)}, u32[]{:S(2)}) %collective-permute-start.9) | collective-permute-done | bytes 30752 | tf_op jit(solution)/shard_map/ppermute | solution.py:637
  61.9 0.8 %sum_far.1 = f32[130,96]{1,0:T(8,128)} custom-call(f32[3,40,128]{2,1,0:T(8,128)S(1)} %get-tuple-element.33.refs_0_, bf16[3,40,128]{2,1,0:T(8,128)(2,1)S(1)} %collective-permute-done.9.refs_1_, bf16[3,40,128]{2,1,0:T(8,128)(2,1)S(1)} %collective-permute-done.10.refs_2_, bf16[3,40,128]{2,1,0:T(8,128)(2,1)S(1)} %collective-permute-done.11.refs_3_), custom_call_target="tpu_custom_call" | custom-call | tf_op jit(solution)/shard_map/sum_far/pallas_call | solution.py:659
  (13 shorter events, 0.1 us)
Async XLA Ops:
  1.9 34.6 %collective-permute-start = (bf16[3,2,128,1024]{3,2,1,0:T(8,128)(2,1)S(1)}, bf16[3,2,128,1024]{3,2,1,0:T(8,128)(2,1)S(1)}, u32[]{:S(2)}, u32[]{:S(2)}) collective-permute-start(bf16[3,2,128,1024]{3,2,1,0:T(8,128)(2,1)S(1)} %bitcast.19), channel_id=1, source_target_pairs={{0,15},{1,0},{2,1},{3,2},{4,3},{5,4},{6,5},{7,6},{8,7},{9,8},{10,9... | collective-permute-start | bytes 4718600 | tf_op jit(solution)/shard_map/ppermute | solution.py:549
  8.9 3.0 %copy-start.1 = (s32[2080]{0:T(1024)S(1)}, s32[2080]{0:T(1024)}, u32[]{:S(2)}) copy-start(s32[2080]{0:T(1024)} %param.5) | copy-start | bytes 24964
  8.9 3.4 %copy-start = (s32[3]{0:T(128)S(1)}, s32[3]{0:T(128)}, u32[]{:S(2)}) copy-start(s32[3]{0:T(128)} %seed_ref.1) | copy-start | bytes 40
  10.0 31.1 %collective-permute-start.1 = (bf16[3,2,64,1024]{3,2,1,0:T(8,128)(2,1)}, bf16[3,2,64,1024]{3,2,1,0:T(8,128)(2,1)}, u32[]{:S(2)}, u32[]{:S(2)}) collective-permute-start(bf16[3,2,64,1024]{3,2,1,0:T(8,128)(2,1)} %bitcast.18.b), channel_id=1, source_target_pairs={{0,15},{1,0},{2,1},{3,2},{4,3},{5,4},{6,5},{7,6},{8,7},{9,8},{10,9... | collective-permute-start | bytes 2359304 | tf_op jit(solution)/shard_map/ppermute | solution.py:549
  11.8 32.6 %collective-permute-start.2 = (bf16[3,2,64,1024]{3,2,1,0:T(8,128)(2,1)}, bf16[3,2,64,1024]{3,2,1,0:T(8,128)(2,1)}, u32[]{:S(2)}, u32[]{:S(2)}) collective-permute-start(bf16[3,2,64,1024]{3,2,1,0:T(8,128)(2,1)} %bitcast.17.c), channel_id=1, source_target_pairs={{0,15},{1,0},{2,1},{3,2},{4,3},{5,4},{6,5},{7,6},{8,7},{9,8},{10,9... | collective-permute-start | bytes 2359304 | tf_op jit(solution)/shard_map/ppermute | solution.py:549
  34.7 16.2 %collective-permute-start.6 = (bf16[4,2,40,128]{3,2,1,0:T(8,128)(2,1)S(1)}, bf16[4,2,40,128]{3,2,1,0:T(8,128)(2,1)S(1)}, u32[]{:S(2)}, u32[]{:S(2)}) collective-permute-start(bf16[4,2,40,128]{3,2,1,0:T(8,128)(2,1)S(1)} %get-tuple-element.30), channel_id=1, source_target_pairs={{0,1},{1,2},{2,3},{3,0},{4,5},{5,6},{6,7},{7,4},{8,9},{9,10},{10,1... | collective-permute-start | bytes 245768 | tf_op jit(solution)/shard_map/ppermute | solution.py:637
  35.4 16.9 %collective-permute-start.7 = (bf16[4,2,40,128]{3,2,1,0:T(8,128)(2,1)S(1)}, bf16[4,2,40,128]{3,2,1,0:T(8,128)(2,1)S(1)}, u32[]{:S(2)}, u32[]{:S(2)}) collective-permute-start(bf16[4,2,40,128]{3,2,1,0:T(8,128)(2,1)S(1)} %get-tuple-element.31), channel_id=1, source_target_pairs={{0,2},{1,3},{2,0},{3,1},{4,6},{5,7},{6,4},{7,5},{8,10},{9,11},{10,... | collective-permute-start | bytes 245768 | tf_op jit(solution)/shard_map/ppermute | solution.py:637
  36.5 15.8 %collective-permute-start.8 = (bf16[4,2,40,128]{3,2,1,0:T(8,128)(2,1)S(1)}, bf16[4,2,40,128]{3,2,1,0:T(8,128)(2,1)S(1)}, u32[]{:S(2)}, u32[]{:S(2)}) collective-permute-start(bf16[4,2,40,128]{3,2,1,0:T(8,128)(2,1)S(1)} %get-tuple-element.32), channel_id=1, source_target_pairs={{0,3},{1,0},{2,1},{3,2},{4,7},{5,4},{6,5},{7,6},{8,11},{9,8},{10,9... | collective-permute-start | bytes 245768 | tf_op jit(solution)/shard_map/ppermute | solution.py:637
  50.2 3.5 %collective-permute-start.3 = (bf16[4,40,128]{2,1,0:T(8,128)(2,1)S(1)}, bf16[4,40,128]{2,1,0:T(8,128)(2,1)S(1)}, u32[]{:S(2)}, u32[]{:S(2)}) collective-permute-start(bf16[4,40,128]{2,1,0:T(8,128)(2,1)S(1)} %get-tuple-element.26), channel_id=1, source_target_pairs={{0,1},{1,2},{2,3},{3,0},{4,5},{5,6},{6,7},{7,4},{8,9},{9,10},{10,1... | collective-permute-start | bytes 122888 | tf_op jit(solution)/shard_map/ppermute | solution.py:637
  50.3 4.3 %collective-permute-start.4 = (bf16[4,40,128]{2,1,0:T(8,128)(2,1)S(1)}, bf16[4,40,128]{2,1,0:T(8,128)(2,1)S(1)}, u32[]{:S(2)}, u32[]{:S(2)}) collective-permute-start(bf16[4,40,128]{2,1,0:T(8,128)(2,1)S(1)} %get-tuple-element.27), channel_id=1, source_target_pairs={{0,2},{1,3},{2,0},{3,1},{4,6},{5,7},{6,4},{7,5},{8,10},{9,11},{10,... | collective-permute-start | bytes 122888 | tf_op jit(solution)/shard_map/ppermute | solution.py:637
  50.9 3.7 %collective-permute-start.5 = (bf16[4,40,128]{2,1,0:T(8,128)(2,1)S(1)}, bf16[4,40,128]{2,1,0:T(8,128)(2,1)S(1)}, u32[]{:S(2)}, u32[]{:S(2)}) collective-permute-start(bf16[4,40,128]{2,1,0:T(8,128)(2,1)S(1)} %get-tuple-element.28), channel_id=1, source_target_pairs={{0,3},{1,0},{2,1},{3,2},{4,7},{5,4},{6,5},{7,6},{8,11},{9,8},{10,9... | collective-permute-start | bytes 122888 | tf_op jit(solution)/shard_map/ppermute | solution.py:637
  54.6 5.2 %collective-permute-start.10 = (bf16[3,40,128]{2,1,0:T(8,128)(2,1)S(1)}, bf16[3,40,128]{2,1,0:T(8,128)(2,1)S(1)}, u32[]{:S(2)}, u32[]{:S(2)}) collective-permute-start(bf16[3,40,128]{2,1,0:T(8,128)(2,1)S(1)} %get-tuple-element.35), channel_id=1, source_target_pairs={{0,8},{1,9},{2,10},{3,11},{4,12},{5,13},{6,14},{7,15},{8,0},{9,1},... | collective-permute-start | bytes 92168 | tf_op jit(solution)/shard_map/ppermute | solution.py:637
  54.7 5.1 %collective-permute-start.11 = (bf16[3,40,128]{2,1,0:T(8,128)(2,1)S(1)}, bf16[3,40,128]{2,1,0:T(8,128)(2,1)S(1)}, u32[]{:S(2)}, u32[]{:S(2)}) collective-permute-start(bf16[3,40,128]{2,1,0:T(8,128)(2,1)S(1)} %get-tuple-element.36), channel_id=1, source_target_pairs={{0,12},{1,13},{2,14},{3,15},{4,0},{5,1},{6,2},{7,3},{8,4},{9,5},{1... | collective-permute-start | bytes 92168 | tf_op jit(solution)/shard_map/ppermute | solution.py:637
  56.1 5.8 %collective-permute-start.9 = (bf16[3,40,128]{2,1,0:T(8,128)(2,1)S(1)}, bf16[3,40,128]{2,1,0:T(8,128)(2,1)S(1)}, u32[]{:S(2)}, u32[]{:S(2)}) collective-permute-start(bf16[3,40,128]{2,1,0:T(8,128)(2,1)S(1)} %get-tuple-element.34), channel_id=1, source_target_pairs={{0,4},{1,5},{2,6},{3,7},{4,8},{5,9},{6,10},{7,11},{8,12},{9,13},{1... | collective-permute-start | bytes 92168 | tf_op jit(solution)/shard_map/ppermute | solution.py:637

commit v2 on v1

--- a/solution.py
+++ b/solution.py
@@ -584,7 +584,7 @@
             pltpu.SemaphoreType.DMA((3, 6)),
             pltpu.SemaphoreType.DMA,
         ],
-        compiler_params=params(40),
+        compiler_params=params(20),
         cost_estimate=cost(6 * flops, 8 * 2**20),
     )(link_seed, where, owners, *own)
     sizes = [count for _, count in chunks]
@@ -605,7 +605,7 @@
             in_specs=[vmem] + [anywhere] * (2 + len(before)),
             out_specs=vmem,
             scratch_shapes=outer_scratch(sizes[which]),
-            compiler_params=params(24),
+            compiler_params=params(20),
             cost_estimate=cost(2**20, 2**18),
         )(links_x, upper[which], left, *before)
 
@@ -625,7 +625,7 @@
             pltpu.VMEM((devices,) + block, BF16),
             pltpu.SemaphoreType.DMA((near,)),
         ],
-        compiler_params=params(24),
+        compiler_params=params(20),
         cost_estimate=cost(2**20, 2**18),
     )(where, owners, first_x, second_x, links_x, upper[2], left)
 

time: 62.9 us -> 62.9 us (level)
  no operation moved by 1% of the time
where the time goes in v2:
time: 62.9 us; the launch traced here: 62.7 us
  Pallas kernels  38.4 us (61%)
  starting transfers between devices  13.6 us (22%)
  waiting for transfers between devices  7.43 us (12%)
  local copies, waits for them, and re-layouts  3.02 us (5%)
    pallas_call x1, Pallas kernels, per_device(): pl.pallas_call(functools.partial(inner_kernel, slots, (near, far)), name=...  22.4 us
    ppermute x9, waiting for transfers between devices, onward(): return lax.ppermute(array, 'sx', [(i, target(i)) for i in range(devices)])  7.42 us
    ppermute x9, starting transfers between devices, onward(): return lax.ppermute(array, 'sx', [(i, target(i)) for i in range(devices)])  7.39 us
    pallas_call x2, Pallas kernels, outer(): pl.pallas_call(kernel, name=name, out_shape=jax.ShapeDtypeStruct(shape, F...  6.51 us
    ppermute x3, starting transfers between devices, per_device(): upper.append(lax.ppermute(part, 'sx', route))  6.19 us
    pallas_call x1, Pallas kernels, per_device(): pl.pallas_call(functools.partial(last_kernel, slots, (near, far)), name='...  5.78 us
    pallas_call x2, Pallas kernels, per_device(): pl.pallas_call(functools.partial(load_kernel, [3 * first for first, _ in...  2.91 us
    reshape x3, local copies, waits for them, and re-layouts, per_device(): part = part.reshape(count, 3, 2, plane).transpose(1, 2, 0, 3)  2.7 us
  transfers between devices with their start and end apart: 12, of which 4 were waited for; matrix products, arithmetic and copies ran while one was open for 4% of the time, Pallas kernels for 58%

profile of v2, /device:TPU:0, one launch (start us, length us, event | category | flops | bytes accessed | tf_op | source)
XLA Modules:
  0.0 62.7 jit_solution(10912459606403622515)
XLA Ops:
  0.0 1.4 %load_modes.2 = bf16[384,2,1024]{2,1,0:T(2,128)(2,1)S(1)} custom-call(bf16[768,2,1024]{2,1,0:T(2,128)(2,1)} %bitcast.27), custom_call_target="tpu_custom_call" | custom-call | bytes 3145728 | tf_op jit(solution)/shard_map/load_modes/pallas_call | solution.py:536
  1.4 0.5 copy.12
  1.9 5.5 %collective-permute-start = (bf16[3,2,128,1024]{3,2,1,0:T(8,128)(2,1)S(1)}, bf16[3,2,128,1024]{3,2,1,0:T(8,128)(2,1)S(1)}, u32[]{:S(2)}, u32[]{:S(2)}) collective-permute-start(bf16[3,2,128,1024]{3,2,1,0:T(8,128)(2,1)S(1)} %bitcast.19), channel_id=1, source_target_pairs={{0,15},{1,0},{2,1},{3,2},{4,3},{5,4},{6,5},{7,6},{8,7},{9,8},{10,9... | collective-permute-start | bytes 4718600 | tf_op jit(solution)/shard_map/ppermute | solution.py:549
  7.3 1.5 %load_modes.3 = (bf16[192,2,1024]{2,1,0:T(2,128)(2,1)S(1)}, bf16[192,2,1024]{2,1,0:T(2,128)(2,1)S(1)}) custom-call(bf16[768,2,1024]{2,1,0:T(2,128)(2,1)} %bitcast.28, bf16[3,2,128,1024]{3,2,1,0:T(8,128)(2,1)S(1)} %bitcast.20), custom_call_target="tpu_custom_call" | custom-call | bytes 3145728 | tf_op jit(solution)/shard_map/load_modes/pallas_call | solution.py:536
  8.9 0.0 copy-start
  8.9 1.1 %copy.14 = bf16[64,3,2,1024]{3,0,2,1:T(8,128)(2,1)} copy(bf16[64,3,2,1024]{3,2,1,0:T(2,128)(2,1)S(1)} %bitcast.24) | data formatting | bytes 1572864 | tf_op jit(solution)/shard_map/reshape | solution.py:547
  10.0 0.7 %collective-permute-start.1 = (bf16[3,2,64,1024]{3,2,1,0:T(8,128)(2,1)}, bf16[3,2,64,1024]{3,2,1,0:T(8,128)(2,1)}, u32[]{:S(2)}, u32[]{:S(2)}) collective-permute-start(bf16[3,2,64,1024]{3,2,1,0:T(8,128)(2,1)} %bitcast.18.b), channel_id=1, source_target_pairs={{0,15},{1,0},{2,1},{3,2},{4,3},{5,4},{6,5},{7,6},{8,7},{9,8},{10,9... | collective-permute-start | bytes 2359304 | tf_op jit(solution)/shard_map/ppermute | solution.py:549
  10.7 1.1 %copy.13 = bf16[64,3,2,1024]{3,0,2,1:T(8,128)(2,1)} copy(bf16[64,3,2,1024]{3,2,1,0:T(2,128)(2,1)S(1)} %bitcast.23) | data formatting | bytes 1572864 | tf_op jit(solution)/shard_map/reshape | solution.py:547
  11.8 0.0 collective-permute-start.2
  11.9 0.1 fusion.11
  11.9 0.1 reshape.25
  12.0 0.1 reshape.26
  12.1 0.1 copy.8
  12.3 22.4 %inner_directions.1 = (bf16[4,2,40,128]{3,2,1,0:T(8,128)(2,1)S(1)}, bf16[4,2,40,128]{3,2,1,0:T(8,128)(2,1)S(1)}, bf16[4,2,40,128]{3,2,1,0:T(8,128)(2,1)S(1)}, bf...) custom-call(s32[3]{0:T(128)S(1)} %copy-done, s32[1]{0:T(128)} %bitcast.where_ref, ...), custom_call_target="tpu_custom_call" | custom-call | flops 9663676416 | bytes 8388608 | tf_op jit(solution)/shard_map/inner_directions/pallas_call | solution.py:565
  34.7 0.7 %collective-permute-start.6 = (bf16[4,2,40,128]{3,2,1,0:T(8,128)(2,1)S(1)}, bf16[4,2,40,128]{3,2,1,0:T(8,128)(2,1)S(1)}, u32[]{:S(2)}, u32[]{:S(2)}) collective-permute-start(bf16[4,2,40,128]{3,2,1,0:T(8,128)(2,1)S(1)} %get-tuple-element.30), channel_id=1, source_target_pairs={{0,1},{1,2},{2,3},{3,0},{4,5},{5,6},{6,7},{7,4},{8,9},{9,10},{10,1... | collective-permute-start | bytes 245768 | tf_op jit(solution)/shard_map/ppermute | solution.py:637
  35.4 1.0 %collective-permute-start.7 = (bf16[4,2,40,128]{3,2,1,0:T(8,128)(2,1)S(1)}, bf16[4,2,40,128]{3,2,1,0:T(8,128)(2,1)S(1)}, u32[]{:S(2)}, u32[]{:S(2)}) collective-permute-start(bf16[4,2,40,128]{3,2,1,0:T(8,128)(2,1)S(1)} %get-tuple-element.31), channel_id=1, source_target_pairs={{0,2},{1,3},{2,0},{3,1},{4,6},{5,7},{6,4},{7,5},{8,10},{9,11},{10,... | collective-permute-start | bytes 245768 | tf_op jit(solution)/shard_map/ppermute | solution.py:637
  36.5 1.4 %collective-permute-start.8 = (bf16[4,2,40,128]{3,2,1,0:T(8,128)(2,1)S(1)}, bf16[4,2,40,128]{3,2,1,0:T(8,128)(2,1)S(1)}, u32[]{:S(2)}, u32[]{:S(2)}) collective-permute-start(bf16[4,2,40,128]{3,2,1,0:T(8,128)(2,1)S(1)} %get-tuple-element.32), channel_id=1, source_target_pairs={{0,3},{1,0},{2,1},{3,2},{4,7},{5,4},{6,5},{7,6},{8,11},{9,8},{10,9... | collective-permute-start | bytes 245768 | tf_op jit(solution)/shard_map/ppermute | solution.py:637
  37.9 3.2 %outer_first.1.before_hbm.first_ref = f32[2,256,128]{2,1,0:T(8,128)S(1)} custom-call(f32[18,8,128]{2,1,0:T(8,128)S(1)} %get-tuple-element.23.links_ref, bf16[3,2,128,1024]{3,2,1,0:T(8,128)(2,1)S(1)} %collective-permute-done.upper_hbm, bf16[512,3072]{1,0:T(8,128)(2,1)S(1)} %get-tuple-element.24.own_hbm), custom_call_target="tpu_custom_call" | custom-call | flops 1048576 | bytes 262144 | tf_op jit(solution)/shard_map/outer_first/pallas_call | solution.py:601
  41.1 3.3 %outer_second.1.second_ref = f32[256,128]{1,0:T(8,128)S(1)} custom-call(f32[18,8,128]{2,1,0:T(8,128)S(1)} %get-tuple-element.23.links_ref, bf16[3,2,64,1024]{3,2,1,0:T(8,128)(2,1)} %collective-permute-done.1.upper_hbm, bf16[512,3072]{1,0:T(8,128)(2,1)S(1)} %get-tuple-element.24.own_hbm, f32[2,256,128]{2,1,0:T(8,128)S(1)} %outer_first.1.before_hbm.first_ref), custom_call_target="tpu_custom_call" | custom-call | flops 1048576 | bytes 262144 | tf_op jit(solution)/shard_map/outer_second/pallas_call | solution.py:601
  44.4 5.8 %outer_last.1 = (bf16[4,40,128]{2,1,0:T(8,128)(2,1)S(1)}, bf16[4,40,128]{2,1,0:T(8,128)(2,1)S(1)}, bf16[4,40,128]{2,1,0:T(8,128)(2,1)S(1)}, bf16[4,40,128]{2,1,0:T(8,128)(2,1)S(1)}) custom-call(s32[1]{0:T(128)} %bitcast.where_ref, s32[160,16]{1,0:T(8,128)S(1)} %bitcast.26, f32[2,256,128]{2,1,0:T(8,128)S(1)} %outer_first.1.before_hbm.first_ref, ...), custom_call_target="tpu_custom_call" | custom-call | flops 1048576 | bytes 262144 | tf_op jit(solution)/shard_map/outer_last/pallas_call | solution.py:614
  50.2 0.1 collective-permute-start.3
  50.3 0.6 %collective-permute-start.4 = (bf16[4,40,128]{2,1,0:T(8,128)(2,1)S(1)}, bf16[4,40,128]{2,1,0:T(8,128)(2,1)S(1)}, u32[]{:S(2)}, u32[]{:S(2)}) collective-permute-start(bf16[4,40,128]{2,1,0:T(8,128)(2,1)S(1)} %get-tuple-element.27), channel_id=1, source_target_pairs={{0,2},{1,3},{2,0},{3,1},{4,6},{5,7},{6,4},{7,5},{8,10},{9,11},{10,... | collective-permute-start | bytes 122888 | tf_op jit(solution)/shard_map/ppermute | solution.py:637
  50.9 1.4 %collective-permute-start.5 = (bf16[4,40,128]{2,1,0:T(8,128)(2,1)S(1)}, bf16[4,40,128]{2,1,0:T(8,128)(2,1)S(1)}, u32[]{:S(2)}, u32[]{:S(2)}) collective-permute-start(bf16[4,40,128]{2,1,0:T(8,128)(2,1)S(1)} %get-tuple-element.28), channel_id=1, source_target_pairs={{0,3},{1,0},{2,1},{3,2},{4,7},{5,4},{6,5},{7,6},{8,11},{9,8},{10,9... | collective-permute-start | bytes 122888 | tf_op jit(solution)/shard_map/ppermute | solution.py:637
  52.3 1.4 %collective-permute-done.3.refs_1_ = bf16[4,40,128]{2,1,0:T(8,128)(2,1)S(1)} collective-permute-done((bf16[4,40,128]{2,1,0:T(8,128)(2,1)S(1)}, bf16[4,40,128]{2,1,0:T(8,128)(2,1)S(1)}, u32[]{:S(2)}, u32[]{:S(2)}) %collective-permute-start.3) | collective-permute-done | bytes 40992 | tf_op jit(solution)/shard_map/ppermute | solution.py:637
  53.7 0.9 %collective-permute-done.4.refs_2_ = bf16[4,40,128]{2,1,0:T(8,128)(2,1)S(1)} collective-permute-done((bf16[4,40,128]{2,1,0:T(8,128)(2,1)S(1)}, bf16[4,40,128]{2,1,0:T(8,128)(2,1)S(1)}, u32[]{:S(2)}, u32[]{:S(2)}) %collective-permute-start.4) | collective-permute-done | bytes 40992 | tf_op jit(solution)/shard_map/ppermute | solution.py:637
  54.6 0.1 sum_near.1
  54.6 0.1 collective-permute-start.10
  54.7 1.4 %collective-permute-start.11 = (bf16[3,40,128]{2,1,0:T(8,128)(2,1)S(1)}, bf16[3,40,128]{2,1,0:T(8,128)(2,1)S(1)}, u32[]{:S(2)}, u32[]{:S(2)}) collective-permute-start(bf16[3,40,128]{2,1,0:T(8,128)(2,1)S(1)} %get-tuple-element.36), channel_id=1, source_target_pairs={{0,12},{1,13},{2,14},{3,15},{4,0},{5,1},{6,2},{7,3},{8,4},{9,5},{1... | collective-permute-start | bytes 92168 | tf_op jit(solution)/shard_map/ppermute | solution.py:637
  56.1 0.7 %collective-permute-start.9 = (bf16[3,40,128]{2,1,0:T(8,128)(2,1)S(1)}, bf16[3,40,128]{2,1,0:T(8,128)(2,1)S(1)}, u32[]{:S(2)}, u32[]{:S(2)}) collective-permute-start(bf16[3,40,128]{2,1,0:T(8,128)(2,1)S(1)} %get-tuple-element.34), channel_id=1, source_target_pairs={{0,4},{1,5},{2,6},{3,7},{4,8},{5,9},{6,10},{7,11},{8,12},{9,13},{1... | collective-permute-start | bytes 92168 | tf_op jit(solution)/shard_map/ppermute | solution.py:637
  56.8 3.0 %collective-permute-done.10.refs_2_ = bf16[3,40,128]{2,1,0:T(8,128)(2,1)S(1)} collective-permute-done((bf16[3,40,128]{2,1,0:T(8,128)(2,1)S(1)}, bf16[3,40,128]{2,1,0:T(8,128)(2,1)S(1)}, u32[]{:S(2)}, u32[]{:S(2)}) %collective-permute-start.10) | collective-permute-done | bytes 30752 | tf_op jit(solution)/shard_map/ppermute | solution.py:637
  59.8 2.1 %collective-permute-done.9.refs_1_ = bf16[3,40,128]{2,1,0:T(8,128)(2,1)S(1)} collective-permute-done((bf16[3,40,128]{2,1,0:T(8,128)(2,1)S(1)}, bf16[3,40,128]{2,1,0:T(8,128)(2,1)S(1)}, u32[]{:S(2)}, u32[]{:S(2)}) %collective-permute-start.9) | collective-permute-done | bytes 30752 | tf_op jit(solution)/shard_map/ppermute | solution.py:637
  61.9 0.8 %sum_far.1 = f32[130,96]{1,0:T(8,128)} custom-call(f32[3,40,128]{2,1,0:T(8,128)S(1)} %get-tuple-element.33.refs_0_, bf16[3,40,128]{2,1,0:T(8,128)(2,1)S(1)} %collective-permute-done.9.refs_1_, bf16[3,40,128]{2,1,0:T(8,128)(2,1)S(1)} %collective-permute-done.10.refs_2_, bf16[3,40,128]{2,1,0:T(8,128)(2,1)S(1)} %collective-permute-done.11.refs_3_), custom_call_target="tpu_custom_call" | custom-call | tf_op jit(solution)/shard_map/sum_far/pallas_call | solution.py:659
  (13 shorter events, 0.1 us)
Async XLA Ops:
  1.9 34.6 %collective-permute-start = (bf16[3,2,128,1024]{3,2,1,0:T(8,128)(2,1)S(1)}, bf16[3,2,128,1024]{3,2,1,0:T(8,128)(2,1)S(1)}, u32[]{:S(2)}, u32[]{:S(2)}) collective-permute-start(bf16[3,2,128,1024]{3,2,1,0:T(8,128)(2,1)S(1)} %bitcast.19), channel_id=1, source_target_pairs={{0,15},{1,0},{2,1},{3,2},{4,3},{5,4},{6,5},{7,6},{8,7},{9,8},{10,9... | collective-permute-start | bytes 4718600 | tf_op jit(solution)/shard_map/ppermute | solution.py:549
  8.9 3.0 %copy-start.1 = (s32[2080]{0:T(1024)S(1)}, s32[2080]{0:T(1024)}, u32[]{:S(2)}) copy-start(s32[2080]{0:T(1024)} %param.5) | copy-start | bytes 24964
  8.9 3.4 %copy-start = (s32[3]{0:T(128)S(1)}, s32[3]{0:T(128)}, u32[]{:S(2)}) copy-start(s32[3]{0:T(128)} %seed_ref.1) | copy-start | bytes 40
  10.0 31.1 %collective-permute-start.1 = (bf16[3,2,64,1024]{3,2,1,0:T(8,128)(2,1)}, bf16[3,2,64,1024]{3,2,1,0:T(8,128)(2,1)}, u32[]{:S(2)}, u32[]{:S(2)}) collective-permute-start(bf16[3,2,64,1024]{3,2,1,0:T(8,128)(2,1)} %bitcast.18.b), channel_id=1, source_target_pairs={{0,15},{1,0},{2,1},{3,2},{4,3},{5,4},{6,5},{7,6},{8,7},{9,8},{10,9... | collective-permute-start | bytes 2359304 | tf_op jit(solution)/shard_map/ppermute | solution.py:549
  11.8 32.6 %collective-permute-start.2 = (bf16[3,2,64,1024]{3,2,1,0:T(8,128)(2,1)}, bf16[3,2,64,1024]{3,2,1,0:T(8,128)(2,1)}, u32[]{:S(2)}, u32[]{:S(2)}) collective-permute-start(bf16[3,2,64,1024]{3,2,1,0:T(8,128)(2,1)} %bitcast.17.c), channel_id=1, source_target_pairs={{0,15},{1,0},{2,1},{3,2},{4,3},{5,4},{6,5},{7,6},{8,7},{9,8},{10,9... | collective-permute-start | bytes 2359304 | tf_op jit(solution)/shard_map/ppermute | solution.py:549
  34.7 16.2 %collective-permute-start.6 = (bf16[4,2,40,128]{3,2,1,0:T(8,128)(2,1)S(1)}, bf16[4,2,40,128]{3,2,1,0:T(8,128)(2,1)S(1)}, u32[]{:S(2)}, u32[]{:S(2)}) collective-permute-start(bf16[4,2,40,128]{3,2,1,0:T(8,128)(2,1)S(1)} %get-tuple-element.30), channel_id=1, source_target_pairs={{0,1},{1,2},{2,3},{3,0},{4,5},{5,6},{6,7},{7,4},{8,9},{9,10},{10,1... | collective-permute-start | bytes 245768 | tf_op jit(solution)/shard_map/ppermute | solution.py:637
  35.4 16.9 %collective-permute-start.7 = (bf16[4,2,40,128]{3,2,1,0:T(8,128)(2,1)S(1)}, bf16[4,2,40,128]{3,2,1,0:T(8,128)(2,1)S(1)}, u32[]{:S(2)}, u32[]{:S(2)}) collective-permute-start(bf16[4,2,40,128]{3,2,1,0:T(8,128)(2,1)S(1)} %get-tuple-element.31), channel_id=1, source_target_pairs={{0,2},{1,3},{2,0},{3,1},{4,6},{5,7},{6,4},{7,5},{8,10},{9,11},{10,... | collective-permute-start | bytes 245768 | tf_op jit(solution)/shard_map/ppermute | solution.py:637
  36.5 15.8 %collective-permute-start.8 = (bf16[4,2,40,128]{3,2,1,0:T(8,128)(2,1)S(1)}, bf16[4,2,40,128]{3,2,1,0:T(8,128)(2,1)S(1)}, u32[]{:S(2)}, u32[]{:S(2)}) collective-permute-start(bf16[4,2,40,128]{3,2,1,0:T(8,128)(2,1)S(1)} %get-tuple-element.32), channel_id=1, source_target_pairs={{0,3},{1,0},{2,1},{3,2},{4,7},{5,4},{6,5},{7,6},{8,11},{9,8},{10,9... | collective-permute-start | bytes 245768 | tf_op jit(solution)/shard_map/ppermute | solution.py:637
  50.2 3.5 %collective-permute-start.3 = (bf16[4,40,128]{2,1,0:T(8,128)(2,1)S(1)}, bf16[4,40,128]{2,1,0:T(8,128)(2,1)S(1)}, u32[]{:S(2)}, u32[]{:S(2)}) collective-permute-start(bf16[4,40,128]{2,1,0:T(8,128)(2,1)S(1)} %get-tuple-element.26), channel_id=1, source_target_pairs={{0,1},{1,2},{2,3},{3,0},{4,5},{5,6},{6,7},{7,4},{8,9},{9,10},{10,1... | collective-permute-start | bytes 122888 | tf_op jit(solution)/shard_map/ppermute | solution.py:637
  50.3 4.3 %collective-permute-start.4 = (bf16[4,40,128]{2,1,0:T(8,128)(2,1)S(1)}, bf16[4,40,128]{2,1,0:T(8,128)(2,1)S(1)}, u32[]{:S(2)}, u32[]{:S(2)}) collective-permute-start(bf16[4,40,128]{2,1,0:T(8,128)(2,1)S(1)} %get-tuple-element.27), channel_id=1, source_target_pairs={{0,2},{1,3},{2,0},{3,1},{4,6},{5,7},{6,4},{7,5},{8,10},{9,11},{10,... | collective-permute-start | bytes 122888 | tf_op jit(solution)/shard_map/ppermute | solution.py:637
  50.9 3.7 %collective-permute-start.5 = (bf16[4,40,128]{2,1,0:T(8,128)(2,1)S(1)}, bf16[4,40,128]{2,1,0:T(8,128)(2,1)S(1)}, u32[]{:S(2)}, u32[]{:S(2)}) collective-permute-start(bf16[4,40,128]{2,1,0:T(8,128)(2,1)S(1)} %get-tuple-element.28), channel_id=1, source_target_pairs={{0,3},{1,0},{2,1},{3,2},{4,7},{5,4},{6,5},{7,6},{8,11},{9,8},{10,9... | collective-permute-start | bytes 122888 | tf_op jit(solution)/shard_map/ppermute | solution.py:637
  54.6 5.2 %collective-permute-start.10 = (bf16[3,40,128]{2,1,0:T(8,128)(2,1)S(1)}, bf16[3,40,128]{2,1,0:T(8,128)(2,1)S(1)}, u32[]{:S(2)}, u32[]{:S(2)}) collective-permute-start(bf16[3,40,128]{2,1,0:T(8,128)(2,1)S(1)} %get-tuple-element.35), channel_id=1, source_target_pairs={{0,8},{1,9},{2,10},{3,11},{4,12},{5,13},{6,14},{7,15},{8,0},{9,1},... | collective-permute-start | bytes 92168 | tf_op jit(solution)/shard_map/ppermute | solution.py:637
  54.7 5.1 %collective-permute-start.11 = (bf16[3,40,128]{2,1,0:T(8,128)(2,1)S(1)}, bf16[3,40,128]{2,1,0:T(8,128)(2,1)S(1)}, u32[]{:S(2)}, u32[]{:S(2)}) collective-permute-start(bf16[3,40,128]{2,1,0:T(8,128)(2,1)S(1)} %get-tuple-element.36), channel_id=1, source_target_pairs={{0,12},{1,13},{2,14},{3,15},{4,0},{5,1},{6,2},{7,3},{8,4},{9,5},{1... | collective-permute-start | bytes 92168 | tf_op jit(solution)/shard_map/ppermute | solution.py:637
  56.1 5.8 %collective-permute-start.9 = (bf16[3,40,128]{2,1,0:T(8,128)(2,1)S(1)}, bf16[3,40,128]{2,1,0:T(8,128)(2,1)S(1)}, u32[]{:S(2)}, u32[]{:S(2)}) collective-permute-start(bf16[3,40,128]{2,1,0:T(8,128)(2,1)S(1)} %get-tuple-element.34), channel_id=1, source_target_pairs={{0,4},{1,5},{2,6},{3,7},{4,8},{5,9},{6,10},{7,11},{8,12},{9,13},{1... | collective-permute-start | bytes 92168 | tf_op jit(solution)/shard_map/ppermute | solution.py:637

commit v3 on v1

--- a/solution.py
+++ b/solution.py
@@ -403,18 +403,21 @@
 
 
 def outer_chunk(links_ref, upper_hbm, own_hbm, vector_ref, left_ref, hop_ref, sems):
-    arriving = load_modes(upper_hbm, vector_ref, sems.at[0], 0)
-    count = left_ref.shape[0] // PIECES
-    own = [
-        pltpu.make_async_copy(
-            own_hbm.at[pl.ds(piece * count, count)],
-            left_ref.at[pl.ds(piece * count, count)],
-            sems.at[1, piece],
-        )
-        for piece in range(PIECES)
-    ]
-    for copy in own:
-        copy.start()
+    arriving = load_modes(upper_hbm, vector_ref, sems.at[3], 0)
+    if len(own_hbm) > 1:
+        own = load_all(own_hbm, left_ref, sems)
+    else:
+        count = left_ref.shape[0] // PIECES
+        own = [
+            pltpu.make_async_copy(
+                own_hbm[0].at[pl.ds(piece * count, count)],
+                left_ref.at[pl.ds(piece * count, count)],
+                sems.at[1, piece],
+            )
+            for piece in range(PIECES)
+        ]
+        for copy in own:
+            copy.start()
     wait_all(arriving)
     hop(vector_ref, hop_ref, links_ref, 0, vector_ref.shape[0] // 2)
     wait_all(own)
@@ -422,12 +425,12 @@
 
 
 def wide_kernel(links_ref, upper_hbm, own_hbm, out_ref, *scratch):
-    out_ref[0], out_ref[1] = outer_chunk(links_ref, upper_hbm, own_hbm, *scratch)
-
-
-def narrow_kernel(links_ref, upper_hbm, own_hbm, before_hbm, out_ref, *scratch):
+    out_ref[0], out_ref[1] = outer_chunk(links_ref, upper_hbm, (own_hbm,), *scratch)
+
+
+def narrow_kernel(links_ref, upper_hbm, a, b, c, before_hbm, out_ref, *scratch):
     del before_hbm
-    out_ref[...] = outer_chunk(links_ref, upper_hbm, own_hbm, *scratch)
+    out_ref[...] = outer_chunk(links_ref, upper_hbm, (a, b, c), *scratch)
 
 
 def last_kernel(
@@ -439,13 +442,15 @@
     second_ref,
     links_ref,
     upper_hbm,
-    own_hbm,
+    a,
+    b,
+    c,
     *refs,
 ):
     near, far = grid
     sent_hbm, refs = refs[:near], refs[near:]
     vector_ref, left_ref, hop_ref, sems, table_ref, fold_ref, chosen_ref, stage_ref, out_sems = refs
-    last = outer_chunk(links_ref, upper_hbm, own_hbm, vector_ref, left_ref, hop_ref, sems)
+    last = outer_chunk(links_ref, upper_hbm, (a, b, c), vector_ref, left_ref, hop_ref, sems)
     quarter = last.shape[1] // 2
     low = iota(last.shape, 1) < quarter
     second = second_ref[...]
@@ -594,28 +599,28 @@
             pltpu.VMEM((2 * size, depth), BF16),
             wide,
             pltpu.VMEM((2 * size, depth), BF16),
-            pltpu.SemaphoreType.DMA((2, 6)),
+            pltpu.SemaphoreType.DMA((4, 6)),
         ]
 
-    def outer(kernel, name, which, shape, before):
+    def outer(kernel, name, which, shape, side):
         return pl.pallas_call(
             kernel,
             name=name,
             out_shape=jax.ShapeDtypeStruct(shape, F32),
-            in_specs=[vmem] + [anywhere] * (2 + len(before)),
+            in_specs=[vmem] + [anywhere] * (1 + len(side)),
             out_specs=vmem,
             scratch_shapes=outer_scratch(sizes[which]),
             compiler_params=params(24),
             cost_estimate=cost(2**20, 2**18),
-        )(links_x, upper[which], left, *before)
-
-    first_x = outer(wide_kernel, "outer_first", 0, (2, modes, sizes[0]), [])
-    second_x = outer(narrow_kernel, "outer_second", 1, (modes, 2 * sizes[1]), [first_x])
+        )(links_x, upper[which], *side)
+
+    first_x = outer(wide_kernel, "outer_first", 0, (2, modes, sizes[0]), [left])
+    second_x = outer(narrow_kernel, "outer_second", 1, (modes, 2 * sizes[1]), own + [first_x])
     sent = pl.pallas_call(
         functools.partial(last_kernel, slots, (near, far)),
         name="outer_last",
         out_shape=[jax.ShapeDtypeStruct((far,) + block, BF16)] * near,
-        in_specs=[smem] + [vmem] * 4 + [anywhere] * 2,
+        in_specs=[smem] + [vmem] * 4 + [anywhere] * 4,
         out_specs=[anywhere] * near,
         scratch_shapes=outer_scratch(sizes[2])
         + [
@@ -627,7 +632,7 @@
         ],
         compiler_params=params(24),
         cost_estimate=cost(2**20, 2**18),
-    )(where, owners, first_x, second_x, links_x, upper[2], left)
+    )(where, owners, first_x, second_x, links_x, upper[2], *own)
 
     def onward(step, array, size, inner):
         def target(i):

time: 62.9 us -> 63.1 us (level)
  local copies, waits for them, and re-layouts: 3.02 us -> 1.19 us
  starting transfers between devices: 13.6 us -> 14.6 us
  Pallas kernels: 38.5 us -> 39.2 us
    reshape x3, local copies, waits for them, and re-layouts: 2.7 us -> 0.87 us  [per_device(): part = part.reshape(count, 3, 2, plane).transpose(1, 2, 0, 3)]
    pallas_call x2, Pallas kernels: 6.53 us -> 7.78 us  [outer(): pl.pallas_call(kernel, name=name, out_shape=jax.ShapeDtypeStruct(shape, F...]
    ppermute x9, starting transfers between devices: 7.38 us -> 8.29 us  [onward(): return lax.ppermute(array, 'sx', [(i, target(i)) for i in range(devices)])]
  transfers between devices with their start and end apart: 12 -> 12, of which waited for: 4 -> 5; matrix products, arithmetic and copies ran while one was open for 4% -> 1% of each run, Pallas kernels for 58% -> 59%
where the time goes in v3:
time: 63.1 us; the launch traced here: 62.8 us
  Pallas kernels  39.2 us (62%)
  starting transfers between devices  14.6 us (23%)
  waiting for transfers between devices  7.59 us (12%)
  local copies, waits for them, and re-layouts  1.19 us (2%)
    pallas_call x1, Pallas kernels, per_device(): pl.pallas_call(functools.partial(inner_kernel, slots, (near, far)), name=...  21.8 us
    ppermute x9, starting transfers between devices, onward(): return lax.ppermute(array, 'sx', [(i, target(i)) for i in range(devices)])  8.29 us
    pallas_call x2, Pallas kernels, outer(): pl.pallas_call(kernel, name=name, out_shape=jax.ShapeDtypeStruct(shape, F...  7.78 us
    ppermute x9, waiting for transfers between devices, onward(): return lax.ppermute(array, 'sx', [(i, target(i)) for i in range(devices)])  7.58 us
    ppermute x3, starting transfers between devices, per_device(): upper.append(lax.ppermute(part, 'sx', route))  6.3 us
    pallas_call x1, Pallas kernels, per_device(): pl.pallas_call(functools.partial(last_kernel, slots, (near, far)), name='...  5.9 us
    pallas_call x2, Pallas kernels, per_device(): pl.pallas_call(functools.partial(load_kernel, [3 * first for first, _ in...  2.91 us
  transfers between devices with their start and end apart: 12, of which 5 were waited for; matrix products, arithmetic and copies ran while one was open for 1% of the time, Pallas kernels for 59%

profile of v3, /device:TPU:0, one launch (start us, length us, event | category | flops | bytes accessed | tf_op | source)
XLA Modules:
  0.0 62.8 jit_solution(12585015573838759748)
XLA Ops:
  0.0 1.4 %load_modes.2 = bf16[384,2,1024]{2,1,0:T(2,128)(2,1)S(1)} custom-call(bf16[768,2,1024]{2,1,0:T(2,128)(2,1)} %bitcast.37), custom_call_target="tpu_custom_call" | custom-call | bytes 3145728 | tf_op jit(solution)/shard_map/load_modes/pallas_call | solution.py:541
  1.4 0.5 copy.12
  1.9 5.5 %collective-permute-start = (bf16[3,2,128,1024]{3,2,1,0:T(8,128)(2,1)S(1)}, bf16[3,2,128,1024]{3,2,1,0:T(8,128)(2,1)}, u32[]{:S(2)}, u32[]{:S(2)}) collective-permute-start(bf16[3,2,128,1024]{3,2,1,0:T(8,128)(2,1)S(1)} %bitcast.19), channel_id=1, source_target_pairs={{0,15},{1,0},{2,1},{3,2},{4,3},{5,4},{6,5},{7,6},{8,7},{9,8},{10,9... | collective-permute-start | bytes 4718600 | tf_op jit(solution)/shard_map/ppermute | solution.py:554
  7.3 1.5 %load_modes.3 = (bf16[192,2,1024]{2,1,0:T(2,128)(2,1)S(1)}, bf16[192,2,1024]{2,1,0:T(2,128)(2,1)S(1)}) custom-call(bf16[768,2,1024]{2,1,0:T(2,128)(2,1)} %bitcast.38, bf16[3,2,128,1024]{3,2,1,0:T(8,128)(2,1)S(1)} %bitcast.20), custom_call_target="tpu_custom_call" | custom-call | bytes 3145728 | tf_op jit(solution)/shard_map/load_modes/pallas_call | solution.py:541
  8.9 0.2 copy.14
  9.1 0.7 %collective-permute-start.1 = (bf16[3,2,64,1024]{3,2,1,0:T(8,128)(2,1)S(1)}, bf16[3,2,64,1024]{3,2,1,0:T(8,128)(2,1)}, u32[]{:S(2)}, u32[]{:S(2)}) collective-permute-start(bf16[3,2,64,1024]{3,2,1,0:T(8,128)(2,1)S(1)} %bitcast.24), channel_id=1, source_target_pairs={{0,15},{1,0},{2,1},{3,2},{4,3},{5,4},{6,5},{7,6},{8,7},{9,8},{10,9... | collective-permute-start | bytes 2359304 | tf_op jit(solution)/shard_map/ppermute | solution.py:554
  9.9 0.2 copy.13
  10.1 0.1 collective-permute-start.2
  10.1 0.1 fusion.11
  10.2 0.1 reshape.25
  10.3 0.1 reshape.26
  10.4 0.1 copy.8
  10.6 21.8 %inner_directions.1 = (bf16[4,2,40,128]{3,2,1,0:T(8,128)(2,1)S(1)}, bf16[4,2,40,128]{3,2,1,0:T(8,128)(2,1)S(1)}, bf16[4,2,40,128]{3,2,1,0:T(8,128)(2,1)S(1)}, bf...) custom-call(s32[3]{0:T(128)S(1)} %copy-done, s32[1]{0:T(128)} %bitcast.where_ref, ...), custom_call_target="tpu_custom_call" | custom-call | flops 9663676416 | bytes 8388608 | tf_op jit(solution)/shard_map/inner_directions/pallas_call | solution.py:570
  32.4 0.7 %collective-permute-start.6 = (bf16[4,2,40,128]{3,2,1,0:T(8,128)(2,1)S(1)}, bf16[4,2,40,128]{3,2,1,0:T(8,128)(2,1)S(1)}, u32[]{:S(2)}, u32[]{:S(2)}) collective-permute-start(bf16[4,2,40,128]{3,2,1,0:T(8,128)(2,1)S(1)} %get-tuple-element.30), channel_id=1, source_target_pairs={{0,1},{1,2},{2,3},{3,0},{4,5},{5,6},{6,7},{7,4},{8,9},{9,10},{10,1... | collective-permute-start | bytes 245768 | tf_op jit(solution)/shard_map/ppermute | solution.py:642
  33.1 1.0 %collective-permute-start.7 = (bf16[4,2,40,128]{3,2,1,0:T(8,128)(2,1)S(1)}, bf16[4,2,40,128]{3,2,1,0:T(8,128)(2,1)S(1)}, u32[]{:S(2)}, u32[]{:S(2)}) collective-permute-start(bf16[4,2,40,128]{3,2,1,0:T(8,128)(2,1)S(1)} %get-tuple-element.31), channel_id=1, source_target_pairs={{0,2},{1,3},{2,0},{3,1},{4,6},{5,7},{6,4},{7,5},{8,10},{9,11},{10,... | collective-permute-start | bytes 245768 | tf_op jit(solution)/shard_map/ppermute | solution.py:642
  34.2 1.4 %collective-permute-start.8 = (bf16[4,2,40,128]{3,2,1,0:T(8,128)(2,1)S(1)}, bf16[4,2,40,128]{3,2,1,0:T(8,128)(2,1)S(1)}, u32[]{:S(2)}, u32[]{:S(2)}) collective-permute-start(bf16[4,2,40,128]{3,2,1,0:T(8,128)(2,1)S(1)} %get-tuple-element.32), channel_id=1, source_target_pairs={{0,3},{1,0},{2,1},{3,2},{4,7},{5,4},{6,5},{7,6},{8,11},{9,8},{10,9... | collective-permute-start | bytes 245768 | tf_op jit(solution)/shard_map/ppermute | solution.py:642
  35.5 4.4 %outer_first.1.before_hbm.first_ref = f32[2,256,128]{2,1,0:T(8,128)S(1)} custom-call(f32[18,8,128]{2,1,0:T(8,128)S(1)} %get-tuple-element.23.links_ref, bf16[3,2,128,1024]{3,2,1,0:T(8,128)(2,1)} %collective-permute-done.upper_hbm, bf16[512,3072]{1,0:T(8,128)(2,1)S(1)} %get-tuple-element.24.own_hbm), custom_call_target="tpu_custom_call" | custom-call | flops 1048576 | bytes 262144 | tf_op jit(solution)/shard_map/outer_first/pallas_call | solution.py:606
  39.9 3.4 %outer_second.1.second_ref = f32[256,128]{1,0:T(8,128)S(1)} custom-call(f32[18,8,128]{2,1,0:T(8,128)S(1)} %get-tuple-element.23.links_ref, bf16[3,2,64,1024]{3,2,1,0:T(8,128)(2,1)} %collective-permute-done.1.upper_hbm, bf16[3,2,128,1024]{3,2,1,0:T(8,128)(2,1)S(1)} %bitcast.22, bf16[3,2,64,1024]{3,2,1,0:T(8,128)(2,1)S(1)} %bitcast.26, ...), custom_call_target="tpu_custom_call" | custom-call | flops 1048576 | bytes 262144 | tf_op jit(solution)/shard_map/outer_second/pallas_call | solution.py:606
  43.4 5.9 %outer_last.1 = (bf16[4,40,128]{2,1,0:T(8,128)(2,1)S(1)}, bf16[4,40,128]{2,1,0:T(8,128)(2,1)S(1)}, bf16[4,40,128]{2,1,0:T(8,128)(2,1)S(1)}, bf16[4,40,128]{2,1,0:T(8,128)(2,1)S(1)}) custom-call(s32[1]{0:T(128)} %bitcast.where_ref, s32[160,16]{1,0:T(8,128)S(1)} %bitcast.36, f32[2,256,128]{2,1,0:T(8,128)S(1)} %outer_first.1.before_hbm.first_ref, ...), custom_call_target="tpu_custom_call" | custom-call | flops 1048576 | bytes 262144 | tf_op jit(solution)/shard_map/outer_last/pallas_call | solution.py:619
  49.3 0.1 collective-permute-start.3
  49.3 0.6 %collective-permute-start.4 = (bf16[4,40,128]{2,1,0:T(8,128)(2,1)S(1)}, bf16[4,40,128]{2,1,0:T(8,128)(2,1)S(1)}, u32[]{:S(2)}, u32[]{:S(2)}) collective-permute-start(bf16[4,40,128]{2,1,0:T(8,128)(2,1)S(1)} %get-tuple-element.27), channel_id=1, source_target_pairs={{0,2},{1,3},{2,0},{3,1},{4,6},{5,7},{6,4},{7,5},{8,10},{9,11},{10,... | collective-permute-start | bytes 122888 | tf_op jit(solution)/shard_map/ppermute | solution.py:642
  50.0 1.4 %collective-permute-start.5 = (bf16[4,40,128]{2,1,0:T(8,128)(2,1)S(1)}, bf16[4,40,128]{2,1,0:T(8,128)(2,1)S(1)}, u32[]{:S(2)}, u32[]{:S(2)}) collective-permute-start(bf16[4,40,128]{2,1,0:T(8,128)(2,1)S(1)} %get-tuple-element.28), channel_id=1, source_target_pairs={{0,3},{1,0},{2,1},{3,2},{4,7},{5,4},{6,5},{7,6},{8,11},{9,8},{10,9... | collective-permute-start | bytes 122888 | tf_op jit(solution)/shard_map/ppermute | solution.py:642
  51.4 1.4 %collective-permute-done.3.refs_1_ = bf16[4,40,128]{2,1,0:T(8,128)(2,1)S(1)} collective-permute-done((bf16[4,40,128]{2,1,0:T(8,128)(2,1)S(1)}, bf16[4,40,128]{2,1,0:T(8,128)(2,1)S(1)}, u32[]{:S(2)}, u32[]{:S(2)}) %collective-permute-start.3) | collective-permute-done | bytes 40992 | tf_op jit(solution)/shard_map/ppermute | solution.py:642
  52.7 0.9 %collective-permute-done.4.refs_2_ = bf16[4,40,128]{2,1,0:T(8,128)(2,1)S(1)} collective-permute-done((bf16[4,40,128]{2,1,0:T(8,128)(2,1)S(1)}, bf16[4,40,128]{2,1,0:T(8,128)(2,1)S(1)}, u32[]{:S(2)}, u32[]{:S(2)}) %collective-permute-start.4) | collective-permute-done | bytes 40992 | tf_op jit(solution)/shard_map/ppermute | solution.py:642
  53.6 0.1 sum_near.1
  53.7 0.8 %collective-permute-start.10 = (bf16[3,40,128]{2,1,0:T(8,128)(2,1)S(1)}, bf16[3,40,128]{2,1,0:T(8,128)(2,1)S(1)}, u32[]{:S(2)}, u32[]{:S(2)}) collective-permute-start(bf16[3,40,128]{2,1,0:T(8,128)(2,1)S(1)} %get-tuple-element.35), channel_id=1, source_target_pairs={{0,8},{1,9},{2,10},{3,11},{4,12},{5,13},{6,14},{7,15},{8,0},{9,1},... | collective-permute-start | bytes 92168 | tf_op jit(solution)/shard_map/ppermute | solution.py:642
  54.5 1.7 %collective-permute-start.11 = (bf16[3,40,128]{2,1,0:T(8,128)(2,1)S(1)}, bf16[3,40,128]{2,1,0:T(8,128)(2,1)S(1)}, u32[]{:S(2)}, u32[]{:S(2)}) collective-permute-start(bf16[3,40,128]{2,1,0:T(8,128)(2,1)S(1)} %get-tuple-element.36), channel_id=1, source_target_pairs={{0,12},{1,13},{2,14},{3,15},{4,0},{5,1},{6,2},{7,3},{8,4},{9,5},{1... | collective-permute-start | bytes 92168 | tf_op jit(solution)/shard_map/ppermute | solution.py:642
  56.2 0.5 collective-permute-start.9
  56.7 2.4 %collective-permute-done.10.refs_2_ = bf16[3,40,128]{2,1,0:T(8,128)(2,1)S(1)} collective-permute-done((bf16[3,40,128]{2,1,0:T(8,128)(2,1)S(1)}, bf16[3,40,128]{2,1,0:T(8,128)(2,1)S(1)}, u32[]{:S(2)}, u32[]{:S(2)}) %collective-permute-start.10) | collective-permute-done | bytes 30752 | tf_op jit(solution)/shard_map/ppermute | solution.py:642
  59.2 0.4 collective-permute-done.11.refs_3_
  59.5 2.5 %collective-permute-done.9.refs_1_ = bf16[3,40,128]{2,1,0:T(8,128)(2,1)S(1)} collective-permute-done((bf16[3,40,128]{2,1,0:T(8,128)(2,1)S(1)}, bf16[3,40,128]{2,1,0:T(8,128)(2,1)S(1)}, u32[]{:S(2)}, u32[]{:S(2)}) %collective-permute-start.9) | collective-permute-done | bytes 30752 | tf_op jit(solution)/shard_map/ppermute | solution.py:642
  62.1 0.8 %sum_far.1 = f32[130,96]{1,0:T(8,128)} custom-call(f32[3,40,128]{2,1,0:T(8,128)S(1)} %get-tuple-element.33.refs_0_, bf16[3,40,128]{2,1,0:T(8,128)(2,1)S(1)} %collective-permute-done.9.refs_1_, bf16[3,40,128]{2,1,0:T(8,128)(2,1)S(1)} %collective-permute-done.10.refs_2_, bf16[3,40,128]{2,1,0:T(8,128)(2,1)S(1)} %collective-permute-done.11.refs_3_), custom_call_target="tpu_custom_call" | custom-call | tf_op jit(solution)/shard_map/sum_far/pallas_call | solution.py:664
  (13 shorter events, 0.1 us)
Async XLA Ops:
  1.9 32.3 %collective-permute-start = (bf16[3,2,128,1024]{3,2,1,0:T(8,128)(2,1)S(1)}, bf16[3,2,128,1024]{3,2,1,0:T(8,128)(2,1)}, u32[]{:S(2)}, u32[]{:S(2)}) collective-permute-start(bf16[3,2,128,1024]{3,2,1,0:T(8,128)(2,1)S(1)} %bitcast.19), channel_id=1, source_target_pairs={{0,15},{1,0},{2,1},{3,2},{4,3},{5,4},{6,5},{7,6},{8,7},{9,8},{10,9... | collective-permute-start | bytes 4718600 | tf_op jit(solution)/shard_map/ppermute | solution.py:554
  8.9 1.3 %copy-start.1 = (s32[2080]{0:T(1024)S(1)}, s32[2080]{0:T(1024)}, u32[]{:S(2)}) copy-start(s32[2080]{0:T(1024)} %param.5) | copy-start | bytes 24964
  8.9 1.7 %copy-start = (s32[3]{0:T(128)S(1)}, s32[3]{0:T(128)}, u32[]{:S(2)}) copy-start(s32[3]{0:T(128)} %seed_ref.1) | copy-start | bytes 40
  9.1 30.8 %collective-permute-start.1 = (bf16[3,2,64,1024]{3,2,1,0:T(8,128)(2,1)S(1)}, bf16[3,2,64,1024]{3,2,1,0:T(8,128)(2,1)}, u32[]{:S(2)}, u32[]{:S(2)}) collective-permute-start(bf16[3,2,64,1024]{3,2,1,0:T(8,128)(2,1)S(1)} %bitcast.24), channel_id=1, source_target_pairs={{0,15},{1,0},{2,1},{3,2},{4,3},{5,4},{6,5},{7,6},{8,7},{9,8},{10,9... | collective-permute-start | bytes 2359304 | tf_op jit(solution)/shard_map/ppermute | solution.py:554
  10.1 33.3 %collective-permute-start.2 = (bf16[3,2,64,1024]{3,2,1,0:T(8,128)(2,1)S(1)}, bf16[3,2,64,1024]{3,2,1,0:T(8,128)(2,1)}, u32[]{:S(2)}, u32[]{:S(2)}) collective-permute-start(bf16[3,2,64,1024]{3,2,1,0:T(8,128)(2,1)S(1)} %bitcast.28), channel_id=1, source_target_pairs={{0,15},{1,0},{2,1},{3,2},{4,3},{5,4},{6,5},{7,6},{8,7},{9,8},{10,9... | collective-permute-start | bytes 2359304 | tf_op jit(solution)/shard_map/ppermute | solution.py:554
  32.4 17.6 %collective-permute-start.6 = (bf16[4,2,40,128]{3,2,1,0:T(8,128)(2,1)S(1)}, bf16[4,2,40,128]{3,2,1,0:T(8,128)(2,1)S(1)}, u32[]{:S(2)}, u32[]{:S(2)}) collective-permute-start(bf16[4,2,40,128]{3,2,1,0:T(8,128)(2,1)S(1)} %get-tuple-element.30), channel_id=1, source_target_pairs={{0,1},{1,2},{2,3},{3,0},{4,5},{5,6},{6,7},{7,4},{8,9},{9,10},{10,1... | collective-permute-start | bytes 245768 | tf_op jit(solution)/shard_map/ppermute | solution.py:642
  33.1 18.3 %collective-permute-start.7 = (bf16[4,2,40,128]{3,2,1,0:T(8,128)(2,1)S(1)}, bf16[4,2,40,128]{3,2,1,0:T(8,128)(2,1)S(1)}, u32[]{:S(2)}, u32[]{:S(2)}) collective-permute-start(bf16[4,2,40,128]{3,2,1,0:T(8,128)(2,1)S(1)} %get-tuple-element.31), channel_id=1, source_target_pairs={{0,2},{1,3},{2,0},{3,1},{4,6},{5,7},{6,4},{7,5},{8,10},{9,11},{10,... | collective-permute-start | bytes 245768 | tf_op jit(solution)/shard_map/ppermute | solution.py:642
  34.2 17.2 %collective-permute-start.8 = (bf16[4,2,40,128]{3,2,1,0:T(8,128)(2,1)S(1)}, bf16[4,2,40,128]{3,2,1,0:T(8,128)(2,1)S(1)}, u32[]{:S(2)}, u32[]{:S(2)}) collective-permute-start(bf16[4,2,40,128]{3,2,1,0:T(8,128)(2,1)S(1)} %get-tuple-element.32), channel_id=1, source_target_pairs={{0,3},{1,0},{2,1},{3,2},{4,7},{5,4},{6,5},{7,6},{8,11},{9,8},{10,9... | collective-permute-start | bytes 245768 | tf_op jit(solution)/shard_map/ppermute | solution.py:642
  49.3 3.5 %collective-permute-start.3 = (bf16[4,40,128]{2,1,0:T(8,128)(2,1)S(1)}, bf16[4,40,128]{2,1,0:T(8,128)(2,1)S(1)}, u32[]{:S(2)}, u32[]{:S(2)}) collective-permute-start(bf16[4,40,128]{2,1,0:T(8,128)(2,1)S(1)} %get-tuple-element.26), channel_id=1, source_target_pairs={{0,1},{1,2},{2,3},{3,0},{4,5},{5,6},{6,7},{7,4},{8,9},{9,10},{10,1... | collective-permute-start | bytes 122888 | tf_op jit(solution)/shard_map/ppermute | solution.py:642
  49.3 4.3 %collective-permute-start.4 = (bf16[4,40,128]{2,1,0:T(8,128)(2,1)S(1)}, bf16[4,40,128]{2,1,0:T(8,128)(2,1)S(1)}, u32[]{:S(2)}, u32[]{:S(2)}) collective-permute-start(bf16[4,40,128]{2,1,0:T(8,128)(2,1)S(1)} %get-tuple-element.27), channel_id=1, source_target_pairs={{0,2},{1,3},{2,0},{3,1},{4,6},{5,7},{6,4},{7,5},{8,10},{9,11},{10,... | collective-permute-start | bytes 122888 | tf_op jit(solution)/shard_map/ppermute | solution.py:642
  50.0 3.6 %collective-permute-start.5 = (bf16[4,40,128]{2,1,0:T(8,128)(2,1)S(1)}, bf16[4,40,128]{2,1,0:T(8,128)(2,1)S(1)}, u32[]{:S(2)}, u32[]{:S(2)}) collective-permute-start(bf16[4,40,128]{2,1,0:T(8,128)(2,1)S(1)} %get-tuple-element.28), channel_id=1, source_target_pairs={{0,3},{1,0},{2,1},{3,2},{4,7},{5,4},{6,5},{7,6},{8,11},{9,8},{10,9... | collective-permute-start | bytes 122888 | tf_op jit(solution)/shard_map/ppermute | solution.py:642
  53.7 5.5 %collective-permute-start.10 = (bf16[3,40,128]{2,1,0:T(8,128)(2,1)S(1)}, bf16[3,40,128]{2,1,0:T(8,128)(2,1)S(1)}, u32[]{:S(2)}, u32[]{:S(2)}) collective-permute-start(bf16[3,40,128]{2,1,0:T(8,128)(2,1)S(1)} %get-tuple-element.35), channel_id=1, source_target_pairs={{0,8},{1,9},{2,10},{3,11},{4,12},{5,13},{6,14},{7,15},{8,0},{9,1},... | collective-permute-start | bytes 92168 | tf_op jit(solution)/shard_map/ppermute | solution.py:642
  54.5 5.0 %collective-permute-start.11 = (bf16[3,40,128]{2,1,0:T(8,128)(2,1)S(1)}, bf16[3,40,128]{2,1,0:T(8,128)(2,1)S(1)}, u32[]{:S(2)}, u32[]{:S(2)}) collective-permute-start(bf16[3,40,128]{2,1,0:T(8,128)(2,1)S(1)} %get-tuple-element.36), channel_id=1, source_target_pairs={{0,12},{1,13},{2,14},{3,15},{4,0},{5,1},{6,2},{7,3},{8,4},{9,5},{1... | collective-permute-start | bytes 92168 | tf_op jit(solution)/shard_map/ppermute | solution.py:642
  56.2 5.8 %collective-permute-start.9 = (bf16[3,40,128]{2,1,0:T(8,128)(2,1)S(1)}, bf16[3,40,128]{2,1,0:T(8,128)(2,1)S(1)}, u32[]{:S(2)}, u32[]{:S(2)}) collective-permute-start(bf16[3,40,128]{2,1,0:T(8,128)(2,1)S(1)} %get-tuple-element.34), channel_id=1, source_target_pairs={{0,4},{1,5},{2,6},{3,7},{4,8},{5,9},{6,10},{7,11},{8,12},{9,13},{1... | collective-permute-start | bytes 92168 | tf_op jit(solution)/shard_map/ppermute | solution.py:642
